TPU v7x, 32 devices: a whole 2x2x4 slice. The times are simulated.
32 devices in a mesh: rep: 2 (over core), shard: 8 (over z, y), seq: 2 (over x).
Axes of the slice: x: 2, y: 2, z: 4, core: 2. Of those that a mesh axis runs over, the one named last changes fastest.
Arguments:
- latents: bfloat16 [16, 1024, 768], P(('rep', 'shard'), 'seq'), may hold values from -6 to 6
- image_loads: int32 [16], P(('rep', 'shard')), may hold values from 0 to 1, as said below
- timesteps: int32 [16], P(('rep', 'shard')), may hold values from 0 to 999
- classes: int32 [16], P(('rep', 'shard')), may hold values from 0 to 999
- label_table: bfloat16 [1000, 768], replicated, may hold values from -6 to 6
- ada_weight: bfloat16 [2, 768, 4608], P(None, 'shard'), may hold values from -0.21875 to 0.21875
- ada_bias: bfloat16 [2, 4608], P(None, 'shard'), may hold values from -3 to 3
- qkv_weight: bfloat16 [2, 768, 2304], P(None, 'shard'), may hold values from -0.21875 to 0.21875
- qv_bias: bfloat16 [2, 1536], P(None, 'shard'), may hold values from -3 to 3
- proj_weight: bfloat16 [2, 768, 768], P(None, 'shard'), may hold values from -0.625 to 0.625
- proj_bias: bfloat16 [2, 768], P(None, 'shard'), may hold values from -3 to 3
- fc1_weight: bfloat16 [2, 768, 3072], P(None, 'shard'), may hold values from -0.21875 to 0.21875
- fc1_bias: bfloat16 [2, 3072], P(None, 'shard'), may hold values from -3 to 3
- fc2_weight: bfloat16 [2, 3072, 768], P(None, 'shard'), may hold values from -0.109375 to 0.109375
- fc2_bias: bfloat16 [2, 768], P(None, 'shard'), may hold values from -3 to 3
- cotangent: bfloat16 [16, 1024, 768], P(('rep', 'shard'), 'seq'), may hold values from -6 to 6
Outputs:
- activations: float32 [16, 1024, 768], P(('rep', 'shard'), 'seq')
- latent_grad: float32 [16, 1024, 768], P(('rep', 'shard'), 'seq')
- cond_grad: float32 [16, 768], P(('rep', 'shard'))
- ada_weight_grad: float32 [2, 768, 4608], P(None, 'shard')
- ada_bias_grad: float32 [2, 4608], P(None, 'shard')
- qkv_weight_grad: float32 [2, 768, 2304], P(None, 'shard')
- qv_bias_grad: float32 [2, 1536], P(None, 'shard')
- proj_weight_grad: float32 [2, 768, 768], P(None, 'shard')
- proj_bias_grad: float32 [2, 768], P(None, 'shard')
- fc1_weight_grad: float32 [2, 768, 3072], P(None, 'shard')
- fc1_bias_grad: float32 [2, 3072], P(None, 'shard')
- fc2_weight_grad: float32 [2, 3072, 768], P(None, 'shard')
- fc2_bias_grad: float32 [2, 768], P(None, 'shard')
Inputs may be any that keep to these rules, and one draw needn't show every extreme that they name: Position p holds image_loads[p] live images in its first slots; its other slots of the 1 are empty and give zero outputs. Some position holds 1 live images and some holds none.
All inputs are finite; a program needn't handle non-finite values.
Results may differ from a plain program's by a relative error of at most 0.04.
Values may be sent and summed in bfloat16 or wider, within the bound.
No kernel may reach another device: no remote copies, remote signals or barrier semaphores. Data moves between devices by JAX's collectives and lax.ppermute only.
A program may use at most 320 MiB of HBM per device.

v0:
```python
import functools
import math

import jax
import jax.numpy as jnp
from jax import lax
from jax.experimental import pallas as pl
from jax.experimental.pallas import tpu as pltpu
from jax.sharding import PartitionSpec as P

HEADS = 12
LAYERS = 2
EPSILON = 1e-06
BF16 = jnp.bfloat16
F32 = jnp.float32


def swap_pairs(value, axis):
    return lax.ppermute(value, axis, [(0, 1), (1, 0)])


def swap_layout(value):
    moved = lax.ppermute(value, ("rep", "seq"), [(1, 2), (2, 1)])
    return jnp.where(lax.axis_index("rep") == lax.axis_index("seq"), value, moved)


def cube_pairs(value, axis, bit):
    return lax.ppermute(value, axis, [(at, at ^ bit) for at in range(lax.axis_size(axis))])


def cube_bits(axis):
    return [1 << place for place in range(lax.axis_size(axis).bit_length() - 1)]


def as_is(value):
    return value


def cube_gather(value, axes, tick=as_is):
    value = value[None]
    for axis in reversed(axes):
        for bit in cube_bits(axis):
            other = tick(cube_pairs(value, axis, bit))
            value = jnp.where(
                lax.axis_index(axis) & bit == 0,
                jnp.concatenate([value, other]),
                jnp.concatenate([other, value]),
            )
    return value


def cube_scatter(value, axis, tick=as_is):
    for bit in reversed(cube_bits(axis)):
        low, high = value[:bit], value[bit:]
        first = lax.axis_index(axis) & bit == 0
        other = tick(cube_pairs(jnp.where(first, high, low), axis, bit))
        value = jnp.where(first, low, high) + other
    return value[0]


def ring_order(size):
    half = size // 2
    return [2 * place for place in range(half)] + [2 * place + 1 for place in reversed(range(half))]


def ring_step(value, forward):
    size = lax.axis_size("shard")
    order = ring_order(size)
    step = 1 if forward else size - 1
    return lax.ppermute(
        value, "shard", [(order[at], order[(at + step) % size]) for at in range(size)]
    )


def ring_ids():
    size = lax.axis_size("shard")
    order = ring_order(size)
    places = [order.index(shard) for shard in range(size)]
    place = jnp.array(places, jnp.int32)[lax.axis_index("shard")]
    return jnp.array(order, jnp.int32)[(place + jnp.arange(size, dtype=jnp.int32)) % size]


OFFSETS = (-1, 1, -2, 2, -3, 3, 4)


def place_kernel(where, *refs):
    (own, *rest) = refs[:23]
    out, sem = refs[23:]
    blocks, beside = rest[0:7], rest[7:11]
    core_blocks, core_beside = rest[11:18], rest[18:22]
    rep, seq = where[8], where[9]
    unit = own.shape[1] // 6

    def put(src, shard, row, rows):
        start = pl.multiple_of(row * unit, unit)
        copy = pltpu.make_async_copy(src, out.at[shard, :, pl.ds(start, rows), :], sem)
        copy.start()
        return [copy]

    copies = put(own, where[0], 0, 6 * unit)
    for slot, offset in enumerate(OFFSETS):
        shard = where[offset % 8]
        far = 3 * rep + 2 * (1 - seq)
        copies += put(blocks[slot], shard, 3 * rep + seq, 2 * unit)
        copies += put(beside[slot // 2].at[slot % 2], shard, far, unit)
        far = 3 * (1 - rep) + 2 * (1 - seq)
        copies += put(core_blocks[slot], shard, 3 * (1 - rep) + seq, 2 * unit)
        copies += put(core_beside[slot // 2].at[slot % 2], shard, far, unit)
    for copy in copies:
        copy.wait()


def gather_ring(piece):
    count, rows, width = piece.shape
    shards = lax.axis_size("shard")
    unit = rows // 6
    rep, seq = lax.axis_index("rep"), lax.axis_index("seq")
    mine = lax.dynamic_slice(piece, (0, (3 * rep + seq) * unit, 0), (count, 2 * unit, width))

    def cross(*blocks):
        cut = [
            lax.dynamic_slice(block, (0, seq * unit, 0), (count, unit, width)) for block in blocks
        ]
        return swap_pairs(jnp.stack(cut), "seq")

    def core(block):
        return swap_pairs(block, "rep")

    def around(up, down):
        return ring_step(up, True), ring_step(down, False)

    up1, down1 = yield around(mine, mine)
    up2, down2, x1, *core1 = yield (
        *around(up1, down1), cross(up1, down1), core(up1), core(down1)
    )
    up3, down3, x2, *core2 = yield (
        *around(up2, down2), cross(up2, down2), core(up2), core(down2), core(x1)
    )
    up4, down4, x3, *core3 = yield (
        *around(up3[:, :unit], down3[:, unit:]), cross(up3, down3), core(up3), core(down3), core(x2)
    )
    far = jnp.concatenate([up4, down4], axis=1)
    x4, *core4 = yield (cross(far), core(far), core(x3))
    (core_x4,) = yield (core(x4),)
    parts = [up1, down1, up2, down2, up3, down3, far, x1, x2, x3, x4]
    parts += core1 + core2[:2] + core3[:2] + core4[:1]
    parts += [core2[2], core3[2], core4[1], core_x4]
    where = jnp.concatenate([ring_ids(), jnp.stack([rep, seq]).astype(jnp.int32)])
    anywhere = pl.BlockSpec(memory_space=pl.ANY)
    return pl.pallas_call(
        place_kernel,
        out_shape=jax.ShapeDtypeStruct((shards, count, rows, width), piece.dtype),
        in_specs=[pl.BlockSpec(memory_space=pltpu.SMEM)] + [anywhere] * 23,
        out_specs=pl.BlockSpec(memory_space=pltpu.VMEM),
        compiler_params=pltpu.CompilerParams(vmem_limit_bytes=32 * 2**20),
        scratch_shapes=[pltpu.SemaphoreType.DMA],
        cost_estimate=pl.CostEstimate(
            flops=0, transcendentals=0, bytes_accessed=2 * shards * piece.size * 2
        ),
    )(where, piece, *parts)


def gather_wide(piece, after=None):
    count, rows, width = piece.shape
    copies = lax.axis_size("rep") * lax.axis_size("seq")
    at = lax.axis_index("rep") * lax.axis_size("seq") + lax.axis_index("seq")
    own = lax.dynamic_slice(piece, (at * (count // copies), 0, 0), (count // copies, rows, width))
    if after is not None:
        own, after = lax.optimization_barrier((own, after))
    whole_piece = lax.all_gather(
        own.reshape(-1, width), ("shard", "rep", "seq"), axis=0, tiled=True
    )
    return whole_piece.reshape(-1, count, rows, width), after


def gather_plain(piece, stacked):
    first, parts = stacked
    width = piece.shape[2]
    whole_piece = lax.all_gather(piece, "shard", axis=0, tiled=False)
    flat = whole_piece.transpose(1, 0, 2, 3).reshape(-1, width, width)
    if parts:
        tall = whole_piece[:, first : first + parts].reshape(parts, width, width)
        flat = jnp.concatenate([flat[:first], tall, flat[first + parts :]])
    return flat[None]


def ring_fits(rows):
    return (
        lax.axis_size("shard") == 8
        and lax.axis_size("rep") == 2
        and lax.axis_size("seq") == 2
        and rows % 96 == 0
    )


def add(left, right):
    return (left.astype(F32) + right.astype(F32)).astype(BF16)


def scatter_ring(grads):
    shards, _, rows, width = grads[0].shape
    count = sum(part.shape[1] for part in grads)
    unit = rows // 6
    rep, seq = lax.axis_index("rep"), lax.axis_index("seq")
    ids = ring_ids()

    def half(which):
        cut = [
            lax.dynamic_slice(
                part, (0, 0, 3 * unit * which, 0), (shards, part.shape[1], 3 * unit, width)
            )
            for part in grads
        ]
        return jnp.concatenate(cut, axis=1)

    (got,) = yield (swap_pairs(half(1 - rep), "rep"),)
    paired = add(half(rep), got)

    def block(offset):
        return lax.dynamic_index_in_dim(paired, ids[offset % 8], 0, keepdims=False)

    def send(offsets):
        sent = [
            lax.dynamic_slice(block(offset), (0, 2 * (1 - seq) * unit, 0), (count, unit, width))
            for offset in offsets
        ]
        return swap_pairs(jnp.stack(sent), "seq")

    def join(offset, got):
        kept = lax.dynamic_slice(block(offset), (0, seq * unit, 0), (count, 2 * unit, width))
        zero = jnp.zeros_like(got)
        beside = jnp.where(
            seq == 0,
            jnp.concatenate([got, zero], axis=1),
            jnp.concatenate([zero, got], axis=1),
        )
        return add(kept, beside)

    far, near3 = yield (send((4,)), send((3, -3)))
    far = join(4, far[0])
    up, down, near2 = yield (
        ring_step(far[:, :unit], True),
        ring_step(far[:, unit:], False),
        send((2, -2)),
    )
    up3, down3 = join(3, near3[0]), join(-3, near3[1])
    up = jnp.concatenate([add(up3[:, :unit], up), up3[:, unit:]], axis=1)
    down = jnp.concatenate([down3[:, :unit], add(down3[:, unit:], down)], axis=1)
    up, down, near1 = yield (ring_step(up, True), ring_step(down, False), send((1, -1)))
    up, down, here = yield (
        ring_step(add(join(2, near2[0]), up), True),
        ring_step(add(join(-2, near2[1]), down), False),
        send((0,)),
    )
    up, down = yield (
        ring_step(add(join(1, near1[0]), up), True),
        ring_step(add(join(-1, near1[1]), down), False),
    )
    total = add(join(0, here[0]).astype(F32) + up.astype(F32), down)
    (other,) = yield (swap_pairs(total, "seq"),)
    left, right = jnp.where(seq == 0, total, other), jnp.where(seq == 0, other, total)
    mine = jnp.concatenate(
        [left[:, :unit], add(left[:, unit:], right[:, :unit]), right[:, unit:]], axis=1
    )
    (other,) = yield (swap_pairs(mine, "rep"),)
    return jnp.where(
        rep == 0,
        jnp.concatenate([mine, other], axis=1),
        jnp.concatenate([other, mine], axis=1),
    ).astype(F32)


class Moves:
    def __init__(self, queue=()):
        self.queue = list(queue)
        self.running = []
        self.done = {}
        self.held = True
        if self.queue:
            self.pull()

    def pull(self):
        (key, piece, stacked) = self.queue.pop(0)
        if not ring_fits(piece.shape[1]):
            self.done[key] = gather_plain(piece, stacked)
            return
        if self.running:
            piece, moving = lax.optimization_barrier(
                (piece, [moving for _, _, moving, _ in self.running])
            )
            self.running = [
                (*move[:2], got, move[3]) for move, got in zip(self.running, moving)
            ]
        stages = gather_ring(piece)
        self.running.append((key, stages, next(stages), 1))

    def start(self, key, grads):
        stages = scatter_ring(grads)
        self.running.append((key, stages, next(stages), 9))

    def tick(self, value=None, only=None):
        waiting = [moving for _, _, moving, _ in self.running]
        if value is not None and waiting:
            value, waiting = lax.optimization_barrier((value, waiting))
        still = []
        for (key, stages, _, count), moving in zip(self.running, waiting):
            if only not in (None, key):
                still.append((key, stages, moving, count))
                continue
            try:
                still.append((key, stages, stages.send(moving), count + 1))
            except StopIteration as end:
                self.done[key] = end.value
        self.running = still
        if self.queue and not self.held and all(count > 4 for _, _, _, count in still):
            self.pull()
        return value

    def need(self, key):
        while key not in self.done:
            self.tick(only=key if any(key == move[0] for move in self.running) else None)
        return self.done[key]

    def finish(self, lates):
        step = 0
        while self.running:
            step += 1
            value = self.tick(lates.get(step))
            if step in lates:
                lates[step] = value
        return self.done, lates


def scatter_wide(grads):
    return lax.psum_scatter(
        grads.reshape(-1, grads.shape[-1]),
        ("shard", "rep", "seq"),
        scatter_dimension=0,
        tiled=True,
    )


def scatter_plain(grads):
    owned = lax.psum_scatter(grads.astype(F32), "shard", scatter_dimension=0, tiled=False)
    return lax.psum(owned.astype(BF16), ("rep", "seq")).astype(F32)


def normalize(values):
    centered = values - jnp.mean(values, axis=-1, keepdims=True)
    scale = lax.rsqrt(jnp.mean(centered * centered, axis=-1, keepdims=True) + EPSILON)
    return centered * scale, scale


def norm_back(grad, normal, scale, factor):
    u = grad * (1.0 + factor)
    return (
        u
        - jnp.mean(u, axis=-1, keepdims=True)
        - normal * jnp.mean(u * normal, axis=-1, keepdims=True)
    ) * scale


def time_embed(steps, width):
    half_width = width // 2
    freqs = jnp.exp(-math.log(10000.0) * jnp.arange(half_width, dtype=F32) / half_width)
    angles = steps.astype(F32)[:, None] * freqs[None, :]
    return jnp.concatenate([jnp.cos(angles), jnp.sin(angles)], axis=-1)


def dot(left, right, left_dims, right_dims):
    return lax.dot_general(
        left, right, ((left_dims, right_dims), ((), ())), preferred_element_type=F32
    )


def nt(left, right, **kw):
    return lax.dot_general(left, right, (((1,), (1,)), ((), ())), preferred_element_type=F32, **kw)


def tn(left, right):
    return lax.dot_general(left, right, (((0,), (0,)), ((), ())), preferred_element_type=F32)


def nn(left, right):
    return lax.dot_general(left, right, (((1,), (0,)), ((), ())), preferred_element_type=F32)


def head_mask(values, head, size):
    lanes = lax.broadcasted_iota(jnp.int32, values.shape, 1)
    inside = (lanes >= head * size) & (lanes < (head + 1) * size)
    return jnp.where(inside, values, jnp.zeros_like(values))


def attend_kernel(size, q_ref, own_ref, other_ref, mixed_ref, log_ref):
    pair = q_ref.shape[1] // size
    queries = q_ref[...] * jnp.asarray(size**-0.5, BF16)
    blocks = []
    for head in range(pair):
        query = head_mask(queries, head, size)
        scores = [nt(own_ref[0], query), nt(other_ref[0], query)]
        top = jnp.maximum(*[jnp.max(part, axis=0, keepdims=True) for part in scores])
        expo = [jnp.exp(part - top) for part in scores]
        totals = sum(jnp.sum(part, axis=0, keepdims=True) for part in expo)
        mixed = tn(own_ref[1], expo[0].astype(BF16)) + tn(other_ref[1], expo[1].astype(BF16))
        blocks.append(mixed[head * size : (head + 1) * size] / totals)
        log_ref[0, head : head + 1, :] = top + jnp.log(totals)
    mixed_ref[...] = jnp.transpose(jnp.concatenate(blocks, axis=0)).astype(BF16)


def attend(queries, own_kv, other_kv):
    tokens, width = queries.shape
    pair = 128 // (width // HEADS)
    groups = HEADS // pair
    kv_spec = pl.BlockSpec((2, tokens, 128), lambda group: (0, 0, group))
    token_spec = pl.BlockSpec((tokens, 128), lambda group: (0, group))
    flops = 8 * tokens * tokens * width
    return pl.pallas_call(
        functools.partial(attend_kernel, width // HEADS),
        grid=(groups,),
        in_specs=[token_spec, kv_spec, kv_spec],
        out_specs=(token_spec, pl.BlockSpec((1, pair, tokens), lambda group: (group, 0, 0))),
        out_shape=(
            jax.ShapeDtypeStruct((tokens, width), BF16),
            jax.ShapeDtypeStruct((groups, pair, tokens), F32),
        ),
        compiler_params=pltpu.CompilerParams(vmem_limit_bytes=40 * 2**20),
        cost_estimate=pl.CostEstimate(
            flops=4 * flops, transcendentals=2 * HEADS * tokens**2, bytes_accessed=12 * queries.size
        ),
    )(queries, own_kv, other_kv)


def attend_back_kernel(
    size, q_ref, own_ref, other_ref, grad_ref, mixed_ref, log_ref, dq_ref, down_ref, dother_ref
):
    pair = q_ref.shape[1] // size
    scale = jnp.asarray(size**-0.5, BF16)
    queries = q_ref[...] * scale
    product = grad_ref[...].astype(F32) * mixed_ref[...].astype(F32)
    ones = jnp.ones((8, product.shape[1]), F32)
    grad_queries = []
    grad_kv = {}
    for head in range(pair):
        query, grad = head_mask(queries, head, size), head_mask(grad_ref[...], head, size)
        delta = nt(ones, head_mask(product, head, size), precision=lax.Precision.HIGHEST)[0:1]
        log_total = log_ref[0, head : head + 1, :]
        grad_query = None
        for side, kv_ref in enumerate((own_ref, other_ref)):
            probs = jnp.exp(nt(kv_ref[0], query) - log_total)
            grad_scores = (probs * (nt(kv_ref[1], grad) - delta)).astype(BF16)
            parts = (nn(grad_scores, query), nn(probs.astype(BF16), grad))
            before = grad_kv.get(side)
            grad_kv[side] = parts if before is None else tuple(a + b for a, b in zip(before, parts))
            part = tn(kv_ref[0], grad_scores)[head * size : (head + 1) * size]
            grad_query = part if grad_query is None else grad_query + part
        grad_queries.append(grad_query)
    total = jnp.transpose(jnp.concatenate(grad_queries, axis=0)) * (size**-0.5)
    dq_ref[...] = total.astype(BF16)
    for side, out_ref in enumerate((down_ref, dother_ref)):
        for at in range(2):
            out_ref[at] = grad_kv[side][at].astype(out_ref.dtype)


def attend_back(queries, own_kv, other_kv, grad_mixed, mixed, log_total):
    tokens, width = queries.shape
    pair = 128 // (width // HEADS)
    groups = HEADS // pair
    kv_spec = pl.BlockSpec((2, tokens, 128), lambda group: (0, 0, group))
    token_spec = pl.BlockSpec((tokens, 128), lambda group: (0, group))
    flops = 20 * tokens * tokens * width
    return pl.pallas_call(
        functools.partial(attend_back_kernel, width // HEADS),
        grid=(groups,),
        in_specs=[
            token_spec,
            kv_spec,
            kv_spec,
            token_spec,
            token_spec,
            pl.BlockSpec((1, pair, tokens), lambda group: (group, 0, 0)),
        ],
        out_specs=(token_spec, kv_spec, kv_spec),
        out_shape=(
            jax.ShapeDtypeStruct((tokens, width), BF16),
            jax.ShapeDtypeStruct(own_kv.shape, F32),
            jax.ShapeDtypeStruct(own_kv.shape, BF16),
        ),
        compiler_params=pltpu.CompilerParams(vmem_limit_bytes=40 * 2**20),
        cost_estimate=pl.CostEstimate(
            flops=4 * flops, transcendentals=2 * HEADS * tokens**2, bytes_accessed=24 * queries.size
        ),
    )(queries, own_kv, other_kv, grad_mixed, mixed, log_total)


def params_of(megabytes=48):
    return pltpu.CompilerParams(vmem_limit_bytes=megabytes * 2**20)


def whole(shape):
    return pl.BlockSpec(shape, lambda *at: (0,) * len(shape))


def column_sum(values):
    return jnp.sum(values, axis=0, keepdims=True)


def matrix_at(array, at, moving=True):
    shards, _, rows, width = array.shape
    return pl.BlockSpec(
        (shards, 1, rows, width), lambda part: (0, at + part if moving else at, 0, 0)
    )


def tall_at(array, at, parts):
    shards, _, rows, width = array.shape
    if shards == 1:
        return matrix_at(array, at)
    return pl.BlockSpec((shards // parts, parts, rows, width), lambda part: (part, at // parts, 0, 0))


def square(ref):
    return ref[...].reshape(ref.shape[-1], ref.shape[-1])


def put_square(ref, value):
    ref[...] = value.astype(ref.dtype).reshape(ref.shape)


def project_kernel(stream_ref, mod_ref, weight_ref, bias_ref, normed_ref, q_ref, kv_ref):
    part = pl.program_id(0)

    @pl.when(part == 0)
    def _():
        normal, _ = normalize(stream_ref[...])
        normed_ref[...] = (normal * (1.0 + mod_ref[1:2]) + mod_ref[0:1]).astype(BF16)

    result = (nn(normed_ref[...], square(weight_ref)) + bias_ref[0]).astype(BF16)

    @pl.when(part == 0)
    def _():
        q_ref[...] = result

    @pl.when(part > 0)
    def _():
        kv_ref[0] = result


def project(stream, modulation, weights, bias):
    tokens, width = stream.shape
    return pl.pallas_call(
        project_kernel,
        grid=(3,),
        in_specs=[
            whole((tokens, width)),
            whole((6, width)),
            matrix_at(weights, 0),
            pl.BlockSpec((1, 1, width), lambda part: (part, 0, 0)),
        ],
        out_specs=(
            whole((tokens, width)),
            whole((tokens, width)),
            pl.BlockSpec((1, tokens, width), lambda part: (jnp.maximum(part - 1, 0), 0, 0)),
        ),
        out_shape=(
            jax.ShapeDtypeStruct((tokens, width), BF16),
            jax.ShapeDtypeStruct((tokens, width), BF16),
            jax.ShapeDtypeStruct((2, tokens, width), BF16),
        ),
        compiler_params=params_of(),
        cost_estimate=pl.CostEstimate(
            flops=6 * tokens * width**2, transcendentals=0, bytes_accessed=12 * tokens * width
        ),
    )(stream, modulation, weights, bias)


GELU_SCALE = math.sqrt(2.0 / math.pi)


def gelu_parts(value):
    square = value * value
    tanh = jnp.tanh(GELU_SCALE * value * (1.0 + 0.044715 * square))
    return square, tanh


def mlp_kernel(
    mixed_ref, stream_ref, mod_ref, proj_ref, proj_b_ref, fc1_ref, fc1_b_ref, fc2_ref, fc2_b_ref,
    attn_ref, middle_ref, normed_ref, hidden_ref, active_ref, mlp_ref, result_ref,
):
    part = pl.program_id(0)

    @pl.when(part == 0)
    def _():
        attn_out = nn(mixed_ref[...], square(proj_ref)) + proj_b_ref[...]
        attn_ref[...] = attn_out
        middle = stream_ref[...] + mod_ref[2:3] * attn_out
        middle_ref[...] = middle
        normal, _ = normalize(middle)
        normed_ref[...] = (normal * (1.0 + mod_ref[4:5]) + mod_ref[3:4]).astype(BF16)

    hidden = nn(normed_ref[...], square(fc1_ref)) + fc1_b_ref[0]
    hidden_ref[0] = hidden
    _, tanh = gelu_parts(hidden)
    active = (0.5 * hidden * (1.0 + tanh)).astype(BF16)
    active_ref[0] = active
    product = nn(active, square(fc2_ref))

    @pl.when(part == 0)
    def _():
        mlp_ref[...] = product + fc2_b_ref[...]

    @pl.when(part > 0)
    def _():
        mlp_ref[...] += product

    @pl.when(part == pl.num_programs(0) - 1)
    def _():
        result_ref[...] = middle_ref[...] + mod_ref[5:6] * mlp_ref[...]


def mlp(mixed, stream, modulation, attn_w, weights, proj_b, fc1_b, fc2_b):
    tokens, width = stream.shape
    parts = fc1_b.shape[0]
    token, row = whole((tokens, width)), whole((1, width))
    by_part = lambda rows: pl.BlockSpec((1, rows, width), lambda part: (part, 0, 0))
    shape = lambda *dims: jax.ShapeDtypeStruct(dims[:-1], dims[-1])
    return pl.pallas_call(
        mlp_kernel,
        grid=(parts,),
        in_specs=[
            token, token, whole((6, width)), matrix_at(attn_w, 3, False), row,
            matrix_at(weights, 0), by_part(1), tall_at(weights, parts, parts), row,
        ],
        out_specs=(token, token, token, by_part(tokens), by_part(tokens), token, token),
        out_shape=(
            shape(tokens, width, F32),
            shape(tokens, width, F32),
            shape(tokens, width, BF16),
            shape(parts, tokens, width, F32),
            shape(parts, tokens, width, BF16),
            shape(tokens, width, F32),
            shape(tokens, width, F32),
        ),
        compiler_params=params_of(),
        cost_estimate=pl.CostEstimate(
            flops=(2 + 4 * parts) * tokens * width**2,
            transcendentals=parts * tokens * width,
            bytes_accessed=(20 + 6 * parts) * tokens * width,
        ),
    )(mixed, stream, modulation, attn_w, proj_b, weights, fc1_b, weights, fc2_b)


def mlp_back_kernel(
    grad_ref, mlp_ref, mod_ref, fc2_ref, fc1_ref, hidden_ref, active_ref, normed_ref, middle_ref,
    attn_ref, mixed_ref, proj_ref,
    fc2_g_ref, fc1_g_ref, proj_g_ref, fc1_b_ref, sums_ref, grad_middle_ref, grad_mixed_ref,
    low_ref, total_ref,
):
    part = pl.program_id(0)

    @pl.when(part == 0)
    def _():
        grad = grad_ref[...]
        sums_ref[2:3] = column_sum(grad * mlp_ref[...])
        low = (grad * mod_ref[5:6]).astype(BF16)
        low_ref[...] = low
        sums_ref[4:5] = column_sum(low.astype(F32))

    low = low_ref[...]
    put_square(fc2_g_ref, tn(active_ref[0], low))
    hidden = hidden_ref[0]
    squared, tanh = gelu_parts(hidden)
    slope = 0.5 * (1.0 + tanh) + (0.5 * GELU_SCALE) * hidden * (1.0 - tanh * tanh) * (
        1.0 + (3 * 0.044715) * squared
    )
    grad_hidden = (nt(low, square(fc2_ref)) * slope).astype(BF16)
    fc1_b_ref[0] = column_sum(grad_hidden.astype(F32))
    put_square(fc1_g_ref, tn(normed_ref[...], grad_hidden))
    product = nt(grad_hidden, square(fc1_ref))

    @pl.when(part == 0)
    def _():
        total_ref[...] = product

    @pl.when(part > 0)
    def _():
        total_ref[...] += product

    @pl.when(part == pl.num_programs(0) - 1)
    def _():
        grad_normed = total_ref[...]
        normal, scale = normalize(middle_ref[...])
        sums_ref[0:1] = column_sum(grad_normed)
        sums_ref[1:2] = column_sum(grad_normed * normal)
        grad_middle = grad_ref[...] + norm_back(grad_normed, normal, scale, mod_ref[4:5])
        grad_middle_ref[...] = grad_middle
        sums_ref[3:4] = column_sum(grad_middle * attn_ref[...])
        grad_attn = (grad_middle * mod_ref[2:3]).astype(BF16)
        sums_ref[5:6] = column_sum(grad_attn.astype(F32))
        put_square(proj_g_ref, tn(mixed_ref[...], grad_attn))
        grad_mixed_ref[...] = nt(grad_attn, square(proj_ref)).astype(BF16)


def mlp_back(
    grad, mlp_out, modulation, attn_w, weights, hidden, active, normed, middle, attn_out, mixed
):
    tokens, width = grad.shape
    parts = hidden.shape[0]
    token = whole((tokens, width))
    form = (weights.shape[0], parts) + weights.shape[2:]
    fc_form, proj_form = jax.ShapeDtypeStruct(form, BF16), jax.ShapeDtypeStruct(
        (form[0], 1) + form[2:], BF16
    )
    by_part = lambda rows: pl.BlockSpec((1, rows, width), lambda part: (part, 0, 0))
    shape = lambda *dims: jax.ShapeDtypeStruct(dims[:-1], dims[-1])
    return pl.pallas_call(
        mlp_back_kernel,
        grid=(parts,),
        in_specs=[
            token, token, whole((6, width)), tall_at(weights, parts, parts), matrix_at(weights, 0),
            by_part(tokens), by_part(tokens), token, token, token, token,
            matrix_at(attn_w, 3, False),
        ],
        out_specs=(
            tall_at(fc_form, 0, parts), matrix_at(fc_form, 0), matrix_at(proj_form, 0, False),
            by_part(1), whole((6, width)), token, token,
        ),
        out_shape=(
            fc_form,
            fc_form,
            proj_form,
            shape(parts, 1, width, F32),
            shape(6, width, F32),
            shape(tokens, width, F32),
            shape(tokens, width, BF16),
        ),
        scratch_shapes=[pltpu.VMEM((tokens, width), BF16), pltpu.VMEM((tokens, width), F32)],
        compiler_params=params_of(56),
        cost_estimate=pl.CostEstimate(
            flops=(4 + 8 * parts) * tokens * width**2,
            transcendentals=parts * tokens * width,
            bytes_accessed=(20 + 6 * parts) * tokens * width + 8 * parts * width**2,
        ),
    )(
        grad, mlp_out, modulation, weights, weights, hidden, active, normed, middle, attn_out,
        mixed, attn_w,
    )


def project_back_kernel(
    gq_ref, own_ref, back_ref, normed_ref, weight_ref, stream_ref, mod_ref, middle_ref,
    weight_g_ref, sums_ref, bias_ref, grad_ref, total_ref,
):
    part = pl.program_id(0)

    def step(grad, first):
        put_square(weight_g_ref, tn(normed_ref[...], grad))
        bias_ref[0] = column_sum(grad.astype(F32))
        product = nt(grad, square(weight_ref))
        total_ref[...] = product if first else total_ref[...] + product

    @pl.when(part == 0)
    def _():
        step(gq_ref[...], True)

    @pl.when(part > 0)
    def _():
        step((own_ref[0] + back_ref[0].astype(F32)).astype(BF16), False)

    @pl.when(part == 2)
    def _():
        grad_normed = total_ref[...]
        normal, scale = normalize(stream_ref[...])
        sums_ref[0:1] = column_sum(grad_normed)
        sums_ref[1:2] = column_sum(grad_normed * normal)
        grad_ref[...] = middle_ref[...] + norm_back(grad_normed, normal, scale, mod_ref[1:2])


def project_back(grad_q, grad_own, returned, normed, weights, stream, modulation, grad_middle):
    tokens, width = stream.shape
    token = whole((tokens, width))
    form = jax.ShapeDtypeStruct((weights.shape[0], 3) + weights.shape[2:], BF16)
    kv = pl.BlockSpec((1, tokens, width), lambda part: (jnp.maximum(part - 1, 0), 0, 0))
    return pl.pallas_call(
        project_back_kernel,
        grid=(3,),
        in_specs=[
            token, kv, kv, token, matrix_at(weights, 0), token, whole((6, width)), token,
        ],
        out_specs=(
            matrix_at(form, 0),
            whole((2, width)),
            pl.BlockSpec((1, 1, width), lambda part: (part, 0, 0)),
            token,
        ),
        out_shape=(
            form,
            jax.ShapeDtypeStruct((2, width), F32),
            jax.ShapeDtypeStruct((3, 1, width), F32),
            jax.ShapeDtypeStruct((tokens, width), F32),
        ),
        scratch_shapes=[pltpu.VMEM((tokens, width), F32)],
        compiler_params=params_of(),
        cost_estimate=pl.CostEstimate(
            flops=12 * tokens * width**2,
            transcendentals=0,
            bytes_accessed=24 * tokens * width + 12 * width**2,
        ),
    )(grad_q, grad_own, returned, normed, weights, stream, modulation, grad_middle)


def layer_forward(stream, modulation, biases, moves, attn_w, fetch_mlp):
    qkv_b, proj_b, fc1_b, fc2_b = biases
    normed, queries, own_kv = project(stream, modulation, attn_w, qkv_b)
    moves.held = False
    own_kv = moves.tick(fetch_mlp(own_kv))
    other_kv = moves.tick(swap_pairs(own_kv, "rep"))
    mixed, log_total = attend(queries, own_kv, other_kv)
    mixed = moves.tick(moves.tick(mixed))
    mlp_w = fetch_mlp()
    attn_out, middle, normed_mlp, hidden, active, mlp_out, result = mlp(
        mixed, stream, modulation, attn_w, mlp_w, proj_b, fc1_b, fc2_b
    )
    result = moves.tick(result)
    return result, (
        stream, normed, queries, own_kv, other_kv, mixed, log_total, attn_out, middle, normed_mlp,
        hidden, active, mlp_out, attn_w, mlp_w,
    )


def layer_backward(grad_out, modulation, kept, shards, moves, send_mlp, send_attn):
    (
        stream, normed, queries, own_kv, other_kv, mixed, log_total, attn_out, middle, normed_mlp,
        hidden, active, mlp_out, attn_w, mlp_w,
    ) = kept
    width = stream.shape[-1]
    fc2_g, fc1_g, proj_g, fc1_b, sums, grad_middle, grad_mixed = mlp_back(
        grad_out, mlp_out, modulation, attn_w, mlp_w, hidden, active, normed_mlp, middle, attn_out,
        mixed,
    )
    grad_mixed = moves.tick(grad_mixed)
    grad_mixed = send_mlp(fc1_g, fc2_g, grad_mixed)
    grad_q, grad_own, grad_other = attend_back(
        queries, own_kv, other_kv, grad_mixed, mixed, log_total
    )
    grad_other = moves.tick(grad_other)
    returned = swap_pairs(grad_other, "rep")
    qkv_g, attn_sums, qkv_b, grad_stream = project_back(
        grad_q, grad_own, returned, normed, attn_w, stream, modulation, grad_middle
    )
    grad_stream = moves.tick(grad_stream)
    send_attn(qkv_g, proj_g)
    grad_modulation = jnp.concatenate(
        [attn_sums[0], attn_sums[1], sums[3], sums[0], sums[1], sums[2]]
    )
    query_value = jnp.concatenate([qkv_b[0, 0], qkv_b[2, 0]])
    bias_grads = [
        part.reshape(shards, -1) for part in (query_value, sums[5], fc1_b.reshape(-1), sums[4])
    ]
    return grad_stream, grad_modulation, jnp.concatenate(bias_grads, axis=1)


def columns(matrix, width):
    return jnp.stack(jnp.split(matrix, matrix.shape[1] // width, axis=1))


def uncolumns(blocks):
    return jnp.concatenate(list(blocks), axis=1)


def shards_program(
    latents,
    image_loads,
    timesteps,
    classes,
    label_table,
    ada_weight,
    ada_bias,
    qkv_weight,
    qv_bias,
    proj_weight,
    proj_bias,
    fc1_weight,
    fc1_bias,
    fc2_weight,
    fc2_bias,
    cotangent,
):
    shards = lax.axis_size("shard")
    width = latents.shape[2]
    own_rows = width // shards
    ff_parts = fc1_weight.shape[2] // width
    shard, rep, seq = lax.axis_index("shard"), lax.axis_index("rep"), lax.axis_index("seq")

    rings = ring_fits(own_rows)
    attn_packs, mlp_packs = [], []
    for layer in range(LAYERS):
        fc2_piece = fc2_weight[layer].reshape(ff_parts, own_rows, width)
        mlp_packs.append(jnp.concatenate([columns(fc1_weight[layer], width), fc2_piece]))
        attn_packs.append(
            jnp.concatenate([columns(qkv_weight[layer], width), proj_weight[layer][None]])
        )
    moves = Moves([(layer, attn_packs[layer], (0, 0)) for layer in range(LAYERS)])

    one_hot = (
        classes[:, None] == jnp.arange(label_table.shape[0], dtype=jnp.int32)[None, :]
    ).astype(BF16)
    cond = dot(one_hot, label_table, (1,), (0,)) + time_embed(timesteps, width)
    cond_low = jax.nn.silu(cond).astype(BF16)
    live_own = (image_loads > 0).astype(BF16)
    shared = cube_gather(
        jnp.concatenate([cond_low[0], jnp.broadcast_to(live_own, (128,))]),
        ("rep", "shard"),
        moves.tick,
    )
    live = lax.dynamic_slice(shared, (seq * shards + shard, width), (1, 1)).astype(F32)
    cond_rows = lax.dynamic_slice(
        shared[:, :width], (0, shard * own_rows), (shared.shape[0], own_rows)
    )
    stream = swap_layout(latents[0]).astype(F32)

    mlp_w = []

    def fetch_mlp(layer, ahead=None):
        if not rings:
            if ahead is not None:
                return ahead
            return gather_plain(mlp_packs[layer], (ff_parts, ff_parts))
        if ahead is None:
            return mlp_w[layer]
        if layer + 1 < LAYERS:
            later, (mlp_w[layer], ahead) = gather_wide(mlp_packs[layer + 1], (mlp_w[layer], ahead))
            mlp_w.append(later)
        return ahead

    if rings:
        mlp_w.append(gather_wide(mlp_packs[0])[0])

    small = jnp.concatenate([ada_bias, qv_bias, proj_bias, fc1_bias, fc2_bias], axis=1)
    small = cube_gather(small, ("shard",)).astype(F32)
    ends = [0]
    for bias in (ada_bias, qv_bias, proj_bias, fc1_bias, fc2_bias):
        ends.append(ends[-1] + bias.shape[1])
    biases, ada_b = [], []
    for layer in range(LAYERS):
        full = [small[:, layer, ends[at] : ends[at + 1]].reshape(-1) for at in range(5)]
        ada_b.append(full[0])
        qkv_b = jnp.concatenate([full[1][:width], jnp.zeros((width,), F32), full[1][width:]])
        biases.append(
            (
                qkv_b.reshape(3, 1, width),
                full[2][None],
                full[3].reshape(ff_parts, 1, width),
                full[4][None],
            )
        )

    mine = lax.dynamic_slice(cond_rows, (seq * shards, 0), (shards, own_rows))
    partial = jnp.concatenate(
        [dot(mine, ada_weight[layer], (1,), (0,)) for layer in range(LAYERS)], axis=1
    )
    modulations = cube_scatter(partial, "shard", moves.tick)
    modulations = [
        (modulations.reshape(LAYERS, -1)[layer] + ada_b[layer]).reshape(6, width)
        for layer in range(LAYERS)
    ]

    kept = []
    for layer in range(LAYERS):
        stream, layer_kept = layer_forward(
            stream,
            modulations[layer],
            biases[layer],
            moves,
            moves.need(layer),
            functools.partial(fetch_mlp, layer),
        )
        kept.append(layer_kept)
    moves = Moves()
    activations = swap_layout((stream * live).astype(BF16)).astype(F32)
    grad_stream = swap_layout(cotangent[0]).astype(F32) * live

    shares = []
    done = {}

    def flat(part):
        return part.reshape(part.shape[1], shards, own_rows, width).transpose(1, 0, 2, 3)

    def send_mlp(layer, fc1_g, fc2_g, grad_mixed):
        if not rings:
            tall = fc2_g.reshape(shards, ff_parts, own_rows, width)
            done["mlp", layer] = scatter_plain(jnp.concatenate([flat(fc1_g), tall], axis=1))
        else:
            both = jnp.concatenate([fc1_g, fc2_g], axis=1)
            both, grad_mixed = lax.optimization_barrier((both, grad_mixed))
            shares.append(scatter_wide(both))
        return grad_mixed

    def send_attn(layer, qkv_g, proj_g):
        if rings:
            moves.start(("attn", layer), [qkv_g, proj_g])
        else:
            both = jnp.concatenate([flat(qkv_g), flat(proj_g)], axis=1)
            done["attn", layer] = scatter_plain(both)

    bias_grads = [None] * LAYERS
    ada_w_grads = [None] * LAYERS
    ada_b_grads = [None] * LAYERS
    grad_cond = 0.0
    for layer in reversed(range(LAYERS)):
        grad_stream, grad_mod, bias_grads[layer] = layer_backward(
            grad_stream,
            modulations[layer],
            kept[layer],
            shards,
            moves,
            functools.partial(send_mlp, layer),
            functools.partial(send_attn, layer),
        )
        grad_mod = (grad_mod + swap_pairs(grad_mod, "rep")).astype(BF16)
        all_mod = cube_gather(grad_mod, ("seq", "shard"))
        ada_w_grads[layer] = dot(cond_rows, all_mod, (0,), (0,))
        own_mod = lax.dynamic_slice(
            all_mod, (0, shard * ada_bias.shape[1]), (all_mod.shape[0], ada_bias.shape[1])
        )
        ada_b_grads[layer] = jnp.sum(own_mod.astype(F32), axis=0)
        rep_mod = lax.dynamic_slice(all_mod, (rep * shards, 0), (shards, all_mod.shape[1]))
        grad_cond = grad_cond + dot(rep_mod, ada_weight[layer], (1,), (1,))

    latent_grad = swap_layout(grad_stream.astype(BF16)).astype(F32)
    all_cond = cube_gather(grad_cond, ("shard",))
    grad_cond_low = lax.dynamic_slice(all_cond, (0, shard, 0), (shards, 1, own_rows)).reshape(
        1, width
    )
    _, silu_pull = jax.vjp(jax.nn.silu, cond)
    cond_grad = silu_pull(grad_cond_low)[0]

    bias_total = cube_scatter(jnp.stack(bias_grads, axis=1), "shard")
    bias_total = bias_total + swap_pairs(bias_total, "rep")
    bias_total = bias_total + swap_pairs(bias_total, "seq")
    qv_b, proj_b, fc1_b, fc2_b = [
        bias_total[:, ends[at] - ends[1] : ends[at + 1] - ends[1]] for at in range(1, 5)
    ]
    if rings:
        moved, lates = moves.finish({3: shares[0], 8: shares[1]})
        done.update(moved)
        for layer, step in ((1, 3), (0, 8)):
            spread = cube_gather(lates[step], ("rep", "seq"))
            done["mlp", layer] = spread.reshape(-1, own_rows, width).astype(F32)
    weight_grads = []
    for layer in range(LAYERS):
        attn_grads, mlp_grads = done["attn", layer], done["mlp", layer]
        weight_grads.append(
            (
                uncolumns(attn_grads[:3]),
                attn_grads[3],
                uncolumns(mlp_grads[:ff_parts]),
                mlp_grads[ff_parts:].reshape(ff_parts * own_rows, width),
            )
        )
    qkv_g, proj_g, fc1_g, fc2_g = [
        jnp.stack([weight_grads[layer][at] for layer in range(LAYERS)]) for at in range(4)
    ]
    return (
        activations[None],
        latent_grad[None],
        cond_grad,
        jnp.stack(ada_w_grads),
        jnp.stack(ada_b_grads),
        qkv_g,
        qv_b,
        proj_g,
        proj_b,
        fc1_g,
        fc1_b,
        fc2_g,
        fc2_b,
    )


def solution(mesh):
    tokens = P(("rep", "shard"), "seq", None)
    images = P(("rep", "shard"))
    matrix = P(None, "shard", None)
    vector = P(None, "shard")
    return jax.shard_map(
        shards_program,
        mesh=mesh,
        in_specs=(tokens, images, images, images, P())
        + (matrix, vector) * 5
        + (tokens,),
        out_specs=(tokens, tokens, P(("rep", "shard"), None)) + (matrix, vector) * 5,
        check_vma=False,
    )
```

profile of v0, /device:TPU:0, one launch (start us, length us, event | category | flops | bytes accessed | tf_op | source)
XLA Modules:
  0.0 674.5 jit_solution(8592123760418989357)
XLA Ops:
  18.2 3.1 collective-permute-start.2
  35.6 4.2 collective-permute-done.4
  50.0 3.0 collective-permute-start.10
  53.4 5.6 collective-permute-done.10
  61.2 4.9 collective-permute-done.12.refs_6_
  66.8 4.4 collective-permute-start.18
  76.6 5.1 collective-permute-start.19
  92.3 3.7 collective-permute-start.24
  99.6 5.4 collective-permute-done.25.refs_11_
  105.2 6.6 collective-permute-start.28
  123.4 5.8 shard_map.328
  135.7 3.6 collective-permute-done.35.refs_1_
  143.6 13.5 %shard_map.329 = (bf16[512,768]{1,0:T(8,128)(2,1)S(1)}, f32[6,2,512]{2,1,0:T(2,128)S(1)}) custom-call(bf16[512,768]{1,0:T(8,128)(2,1)S(1)} %copy-done.88, bf16[2,512,768]{2,1,0:T(8,128)(2,1)} %get-tuple-element.172.own_ref, bf16[2,512,768]{2,1,0:T(8,128)(2,1)} %collective-permute-done.34.other_ref), custom_call_target="tpu_custom_call" | custom-call | flops 6442450944 | bytes 4718592 | tf_op jit(solution)/shard_map/pallas_call | solution.py:417
  162.7 6.0 collective-permute-done.42.refs_5_
  170.3 3.7 collective-permute-done.43.refs_6_
  180.5 14.6 %shard_map.330 = (f32[512,768]{1,0:T(8,128)S(1)}, f32[512,768]{1,0:T(8,128)S(1)}, bf16[512,768]{1,0:T(8,128)(2,1)S(1)}, f32[4,512,768]{2,1,0:T(8,128)}, bf16[4,5...) custom-call(bf16[512,768]{1,0:T(8,128)(2,1)S(1)} %get-tuple-element.181.mixed_ref, ...), custom_call_target="tpu_custom_call" | custom-call | flops 5435817984 | bytes 17301504 | tf_op jit(solution)/shard_map/pallas_call | solution.py:626
  199.6 3.0 collective-permute-start.54
  202.6 5.5 collective-permute-done.54.refs_11_
  221.6 3.0 shard_map.331.weight_ref.proj_ref
  226.9 5.7 shard_map.332
  239.0 13.5 %shard_map.333 = (bf16[512,768]{1,0:T(8,128)(2,1)S(1)}, f32[6,2,512]{2,1,0:T(2,128)S(1)}) custom-call(bf16[512,768]{1,0:T(8,128)(2,1)S(1)} %copy-done.91, bf16[2,512,768]{2,1,0:T(8,128)(2,1)} %get-tuple-element.200.own_ref, bf16[2,512,768]{2,1,0:T(8,128)(2,1)} %collective-permute-done.58.other_ref), custom_call_target="tpu_custom_call" | custom-call | flops 6442450944 | bytes 4718592 | tf_op jit(solution)/shard_map/pallas_call | solution.py:417
  252.5 14.6 %shard_map.334 = (f32[512,768]{1,0:T(8,128)S(1)}, f32[512,768]{1,0:T(8,128)S(1)}, bf16[512,768]{1,0:T(8,128)(2,1)S(1)}, f32[4,512,768]{2,1,0:T(8,128)}, bf16[4,5...) custom-call(bf16[512,768]{1,0:T(8,128)(2,1)S(1)} %get-tuple-element.201.mixed_ref, ...), custom_call_target="tpu_custom_call" | custom-call | flops 5435817984 | bytes 17301504 | tf_op jit(solution)/shard_map/pallas_call | solution.py:626
  270.5 24.3 %shard_map.335 = (bf16[8,4,96,768]{3,2,1,0:T(8,128)(2,1)}, bf16[8,4,96,768]{3,2,1,0:T(8,128)(2,1)}, bf16[8,1,96,768]{3,2,1,0:T(8,128)(2,1)}, f32[4,1,768]{2,1,0:...) custom-call(f32[512,768]{1,0:T(8,128)} %convert_multiply_fusion.grad_ref, ...), custom_call_target="tpu_custom_call" | custom-call | flops 10871635968 | bytes 36175872 | tf_op jit(solution)/shard_map/pallas_call | solution.py:715
  294.8 7.7 %pad_maximum_fusion = bf16[8,8,96,768]{3,2,1,0:T(8,128)(2,1)} fusion(bf16[8,4,96,768]{3,2,1,0:T(8,128)(2,1)} %get-tuple-element.211, bf16[8,4,96,768]{3,2,1,0:T(8,128)(2,1)} %get-tuple-element.210), kind=kLoop, calls=%fused_computation.1 | loop fusion | flops 4718592 | bytes 18874368 | tf_op jit(solution)/shard_map/concatenate | solution.py:993
  304.9 23.2 %shard_map.336 = (bf16[512,768]{1,0:T(8,128)(2,1)S(1)}, f32[2,512,768]{2,1,0:T(8,128)S(1)}, bf16[2,512,768]{2,1,0:T(8,128)(2,1)}) custom-call(bf16[512,768]{1,0:T(8,128)(2,1)S(1)} %copy-done.92, bf16[2,512,768]{2,1,0:T(8,128)(2,1)} %get-tuple-element.200.own_ref, bf16[2,512,768]{2,1,0:T(8,128)(2,1)} %collective-permute-done.58.other_ref, ...), custom_call_target="tpu_custom_call" | custom-call | flops 16106127360 | bytes 9437184 | tf_op jit(solution)/shard_map/pallas_call | solution.py:471
  329.8 11.0 %collective-permute-start.61 = (bf16[2,512,768]{2,1,0:T(8,128)(2,1)}, bf16[2,512,768]{2,1,0:T(8,128)(2,1)S(1)}, u32[]{:S(2)}, u32[]{:S(2)}) collective-permute-start(bf16[2,512,768]{2,1,0:T(8,128)(2,1)} %get-tuple-element.217), channel_id=1, source_target_pairs={{0,16},{16,0},{1,17},{17,1},{2,18},{18,2},{3,19},{19,3},{4,20},{20... | collective-permute-start | bytes 4718600 | tf_op jit(solution)/shard_map/ppermute | solution.py:19
  362.9 10.4 %shard_map.337 = (bf16[8,3,96,768]{3,2,1,0:T(8,128)(2,1)}, f32[2,768]{1,0:T(2,128)S(1)}, f32[3,1,768]{2,1,0:T(1,128)S(1)}, f32[512,768]{1,0:T(8,128)S(1)}) custom-call(bf16[512,768]{1,0:T(8,128)(2,1)S(1)} %get-tuple-element.215.gq_ref, f32[2,512,768]{2,1,0:T(8,128)} %copy-done.6, bf16[2,512,768]{2,1,0:T(8,128)(2,1)S(1)} %collective-permute-done.61.back_ref, ...), custom_call_target="tpu_custom_call" | custom-call | flops 3623878656 | bytes 16515072 | tf_op jit(solution)/shard_map/pallas_call | solution.py:783
  380.6 24.4 %shard_map.338 = (bf16[8,4,96,768]{3,2,1,0:T(8,128)(2,1)}, bf16[8,4,96,768]{3,2,1,0:T(8,128)(2,1)}, bf16[8,1,96,768]{3,2,1,0:T(8,128)(2,1)}, f32[4,1,768]{2,1,0:...) custom-call(f32[512,768]{1,0:T(8,128)} %copy-done.14, ...), custom_call_target="tpu_custom_call" | custom-call | flops 10871635968 | bytes 36175872 | tf_op jit(solution)/shard_map/pallas_call | solution.py:715
  405.1 8.0 %pad_maximum_fusion.1 = bf16[8,8,96,768]{3,2,1,0:T(8,128)(2,1)} fusion(bf16[8,4,96,768]{3,2,1,0:T(8,128)(2,1)} %get-tuple-element.228, bf16[8,4,96,768]{3,2,1,0:T(8,128)(2,1)} %get-tuple-element.227), kind=kLoop, calls=%fused_computation.2 | loop fusion | flops 4718592 | bytes 18874368 | tf_op jit(solution)/shard_map/concatenate | solution.py:993
  415.6 2.9 collective-permute-done.71
  418.6 2.9 collective-permute-start.72
  423.5 3.6 collective-permute-start.73
  433.5 3.8 add_convert_fusion.1
  441.7 22.7 %shard_map.339 = (bf16[512,768]{1,0:T(8,128)(2,1)S(1)}, f32[2,512,768]{2,1,0:T(8,128)S(1)}, bf16[2,512,768]{2,1,0:T(8,128)(2,1)S(1)}) custom-call(bf16[512,768]{1,0:T(8,128)(2,1)S(1)} %copy-done.89, bf16[2,512,768]{2,1,0:T(8,128)(2,1)} %get-tuple-element.172.own_ref, bf16[2,512,768]{2,1,0:T(8,128)(2,1)} %collective-permute-done.34.other_ref, ...), custom_call_target="tpu_custom_call" | custom-call | flops 16106127360 | bytes 9437184 | tf_op jit(solution)/shard_map/pallas_call | solution.py:471
  478.5 5.8 collective-permute-done.86
  486.0 10.3 %shard_map.340 = (bf16[8,3,96,768]{3,2,1,0:T(8,128)(2,1)}, f32[2,768]{1,0:T(2,128)S(1)}, f32[3,1,768]{2,1,0:T(1,128)S(1)}, f32[512,768]{1,0:T(8,128)S(1)}) custom-call(bf16[512,768]{1,0:T(8,128)(2,1)S(1)} %copy-done.20, f32[2,512,768]{2,1,0:T(8,128)} %copy-done.7, bf16[2,512,768]{2,1,0:T(8,128)(2,1)S(1)} %collective-permute-done.65.back_ref, ...), custom_call_target="tpu_custom_call" | custom-call | flops 3623878656 | bytes 16515072 | tf_op jit(solution)/shard_map/pallas_call | solution.py:783
  504.9 3.8 constant_dynamic-slice_fusion.14
  540.8 14.7 %collective-permute-done.82 = f32[4,8,96]{2,1,0:T(8,128)S(1)} collective-permute-done((f32[4,8,96]{2,1,0:T(8,128)S(1)}, f32[4,8,96]{2,1,0:T(8,128)S(1)}, u32[]{:S(2)}, u32[]{:S(2)}) %collective-permute-start.82) | collective-permute-done | bytes 12320 | tf_op jit(solution)/shard_map/ppermute | solution.py:28
  559.7 8.2 %collective-permute-done.87 = bf16[4,32,768]{2,1,0:T(8,128)(2,1)S(1)} collective-permute-done((bf16[4,32,768]{2,1,0:T(8,128)(2,1)S(1)}, bf16[4,32,768]{2,1,0:T(8,128)(2,1)S(1)}, u32[]{:S(2)}, u32[]{:S(2)}) %collective-permute-start.87) | collective-permute-done | bytes 196640 | tf_op jit(solution)/shard_map/ppermute | solution.py:70
  570.3 4.4 collective-permute-done.88
  581.5 8.7 %collective-permute-done.97 = bf16[2,4,16,768]{3,2,1,0:T(8,128)(2,1)S(1)} collective-permute-done((bf16[2,4,16,768]{3,2,1,0:T(8,128)(2,1)S(1)}, bf16[2,4,16,768]{3,2,1,0:T(8,128)(2,1)S(1)}, u32[]{:S(2)}, u32[]{:S(2)}) %collective-permute-start.97) | collective-permute-done | bytes 196640 | tf_op jit(solution)/shard_map/ppermute | solution.py:19
  594.7 4.3 collective-permute-done.85
  608.0 8.4 %collective-permute-done.98 = bf16[4,32,768]{2,1,0:T(8,128)(2,1)S(1)} collective-permute-done((bf16[4,32,768]{2,1,0:T(8,128)(2,1)S(1)}, bf16[4,32,768]{2,1,0:T(8,128)(2,1)S(1)}, u32[]{:S(2)}, u32[]{:S(2)}) %collective-permute-start.98) | collective-permute-done | bytes 196640 | tf_op jit(solution)/shard_map/ppermute | solution.py:70
  617.8 4.9 collective-permute-done.99
  626.0 3.1 collective-permute-done.101
  632.6 3.5 collective-permute-done.102
  645.8 3.6 collective-permute-done.104
  654.9 6.0 collective-permute-done.114
  (805 shorter events, 267.1 us)
Async XLA Ops:
  7.2 124.4 %all-gather.3.cloned.1.call-start = ((), (), s32[]{:S(2)}) async-start(), calls=%async_computation.2 | async-start | bytes 9732096 | tf_op jit(solution)/shard_map/all_gather | solution.py:170
  15.3 237.2 %all-gather.5.cloned.1.call-start = ((), (), s32[]{:S(2)}) async-start(), calls=%async_computation.3 | async-start | bytes 9732096 | tf_op jit(solution)/shard_map/all_gather | solution.py:170
  18.2 13.1 %collective-permute-start.2 = (bf16[4,32,768]{2,1,0:T(8,128)(2,1)S(1)}, bf16[4,32,768]{2,1,0:T(8,128)(2,1)S(1)}, u32[]{:S(2)}, u32[]{:S(2)}) collective-permute-start(bf16[4,32,768]{2,1,0:T(8,128)(2,1)S(1)} %constant_dynamic-slice_fusion.28), channel_id=1, source_target_pairs={{0,4},{4,8},{8,12},{12,14},{14,10},{10,6},{6,2},{2,0},{1,5},{5,9},... | collective-permute-start | bytes 589832 | tf_op jit(solution)/shard_map/ppermute | solution.py:70
  47.4 13.1 %collective-permute-start.11 = (bf16[4,32,768]{2,1,0:T(8,128)(2,1)S(1)}, bf16[4,32,768]{2,1,0:T(8,128)(2,1)S(1)}, u32[]{:S(2)}, u32[]{:S(2)}) collective-permute-start(bf16[4,32,768]{2,1,0:T(8,128)(2,1)S(1)} %collective-permute-done.5.refs_3_), channel_id=1, source_target_pairs={{0,4},{4,8},{8,12},{12,14},{14,10},{10,6},{6,2},{2,0},{1,5},{5,9},... | collective-permute-start | bytes 589832 | tf_op jit(solution)/shard_map/ppermute | solution.py:70
  50.0 16.1 %collective-permute-start.14 = (bf16[4,32,768]{2,1,0:T(8,128)(2,1)S(1)}, bf16[4,32,768]{2,1,0:T(8,128)(2,1)S(1)}, u32[]{:S(2)}, u32[]{:S(2)}) collective-permute-start(bf16[4,32,768]{2,1,0:T(8,128)(2,1)S(1)} %collective-permute-done.5.refs_3_), channel_id=1, source_target_pairs={{0,16},{16,0},{1,17},{17,1},{2,18},{18,2},{3,19},{19,3},{4,20},{20... | collective-permute-start | bytes 589832 | tf_op jit(solution)/shard_map/ppermute | solution.py:19
  53.0 13.1 %collective-permute-start.12 = (bf16[4,32,768]{2,1,0:T(8,128)(2,1)S(1)}, bf16[4,32,768]{2,1,0:T(8,128)(2,1)S(1)}, u32[]{:S(2)}, u32[]{:S(2)}) collective-permute-start(bf16[4,32,768]{2,1,0:T(8,128)(2,1)S(1)} %collective-permute-done.6.refs_4_), channel_id=1, source_target_pairs={{0,2},{4,0},{8,4},{12,8},{14,12},{10,14},{6,10},{2,6},{1,3},{5,1},... | collective-permute-start | bytes 589832 | tf_op jit(solution)/shard_map/ppermute | solution.py:70
  66.4 21.7 %collective-permute-start.21 = (bf16[4,32,768]{2,1,0:T(8,128)(2,1)S(1)}, bf16[4,32,768]{2,1,0:T(8,128)(2,1)S(1)}, u32[]{:S(2)}, u32[]{:S(2)}) collective-permute-start(bf16[4,32,768]{2,1,0:T(8,128)(2,1)S(1)} %collective-permute-done.11.refs_5_), channel_id=1, source_target_pairs={{0,16},{16,0},{1,17},{17,1},{2,18},{18,2},{3,19},{19,3},{4,20},{20... | collective-permute-start | bytes 589832 | tf_op jit(solution)/shard_map/ppermute | solution.py:19
  71.2 16.9 %collective-permute-start.22 = (bf16[4,32,768]{2,1,0:T(8,128)(2,1)S(1)}, bf16[4,32,768]{2,1,0:T(8,128)(2,1)S(1)}, u32[]{:S(2)}, u32[]{:S(2)}) collective-permute-start(bf16[4,32,768]{2,1,0:T(8,128)(2,1)S(1)} %collective-permute-done.12.refs_6_), channel_id=1, source_target_pairs={{0,16},{16,0},{1,17},{17,1},{2,18},{18,2},{3,19},{19,3},{4,20},{20... | collective-permute-start | bytes 589832 | tf_op jit(solution)/shard_map/ppermute | solution.py:19
  71.3 16.8 %collective-permute-start.20 = (bf16[2,4,16,768]{3,2,1,0:T(8,128)(2,1)S(1)}, bf16[2,4,16,768]{3,2,1,0:T(8,128)(2,1)S(1)}, u32[]{:S(2)}, u32[]{:S(2)}) collective-permute-start(bf16[2,4,16,768]{3,2,1,0:T(8,128)(2,1)S(1)} %pad_maximum_fusion.15), channel_id=1, source_target_pairs={{0,1},{1,0},{2,3},{3,2},{4,5},{5,4},{6,7},{7,6},{8,9},{9,8},{10,11... | collective-permute-start | bytes 589832 | tf_op jit(solution)/shard_map/ppermute | solution.py:19
  72.7 15.4 %collective-permute-start.23 = (bf16[2,4,16,768]{3,2,1,0:T(8,128)(2,1)S(1)}, bf16[2,4,16,768]{3,2,1,0:T(8,128)(2,1)S(1)}, u32[]{:S(2)}, u32[]{:S(2)}) collective-permute-start(bf16[2,4,16,768]{3,2,1,0:T(8,128)(2,1)S(1)} %collective-permute-done.13.refs_9_), channel_id=1, source_target_pairs={{0,16},{16,0},{1,17},{17,1},{2,18},{18,2},{3,19},{19,3},{4,20},{20... | collective-permute-start | bytes 589832 | tf_op jit(solution)/shard_map/ppermute | solution.py:19
  86.5 29.5 %collective-permute-start = (bf16[512,768]{1,0:T(8,128)(2,1)}, bf16[512,768]{1,0:T(8,128)(2,1)}, u32[]{:S(2)}, u32[]{:S(2)}) collective-permute-start(bf16[512,768]{1,0:T(8,128)(2,1)} %bitcast.281), channel_id=1, source_target_pairs={{1,16},{16,1},{3,18},{18,3},{5,20},{20,5},{7,22},{22,7},{9,24},{24... | collective-permute-start | bytes 2359304 | tf_op jit(solution)/shard_map/ppermute | solution.py:23
  131.6 472.0 %reduce-scatter.3.cloned.1.call-start = ((), (), s32[]{:S(2)}) async-start(), calls=%async_computation.4 | async-start | bytes 9732096 | tf_op jit(solution)/shard_map/reduce_scatter | solution.py:335
  140.9 16.8 %collective-permute-start.37 = (bf16[4,32,768]{2,1,0:T(8,128)(2,1)S(1)}, bf16[4,32,768]{2,1,0:T(8,128)(2,1)S(1)}, u32[]{:S(2)}, u32[]{:S(2)}) collective-permute-start(bf16[4,32,768]{2,1,0:T(8,128)(2,1)S(1)} %collective-permute-done.35.refs_1_), channel_id=1, source_target_pairs={{0,4},{4,8},{8,12},{12,14},{14,10},{10,6},{6,2},{2,0},{1,5},{5,9},... | collective-permute-start | bytes 589832 | tf_op jit(solution)/shard_map/ppermute | solution.py:70
  142.6 15.1 %collective-permute-start.40 = (bf16[4,32,768]{2,1,0:T(8,128)(2,1)S(1)}, bf16[4,32,768]{2,1,0:T(8,128)(2,1)S(1)}, u32[]{:S(2)}, u32[]{:S(2)}) collective-permute-start(bf16[4,32,768]{2,1,0:T(8,128)(2,1)S(1)} %collective-permute-done.35.refs_1_), channel_id=1, source_target_pairs={{0,16},{16,0},{1,17},{17,1},{2,18},{18,2},{3,19},{19,3},{4,20},{20... | collective-permute-start | bytes 589832 | tf_op jit(solution)/shard_map/ppermute | solution.py:19
  142.6 15.1 %collective-permute-start.38 = (bf16[4,32,768]{2,1,0:T(8,128)(2,1)S(1)}, bf16[4,32,768]{2,1,0:T(8,128)(2,1)S(1)}, u32[]{:S(2)}, u32[]{:S(2)}) collective-permute-start(bf16[4,32,768]{2,1,0:T(8,128)(2,1)S(1)} %collective-permute-done.36.refs_2_), channel_id=1, source_target_pairs={{0,2},{4,0},{8,4},{12,8},{14,12},{10,14},{6,10},{2,6},{1,3},{5,1},... | collective-permute-start | bytes 589832 | tf_op jit(solution)/shard_map/ppermute | solution.py:70
  142.9 15.5 %collective-permute-start.41 = (bf16[4,32,768]{2,1,0:T(8,128)(2,1)S(1)}, bf16[4,32,768]{2,1,0:T(8,128)(2,1)S(1)}, u32[]{:S(2)}, u32[]{:S(2)}) collective-permute-start(bf16[4,32,768]{2,1,0:T(8,128)(2,1)S(1)} %collective-permute-done.36.refs_2_), channel_id=1, source_target_pairs={{0,16},{16,0},{1,17},{17,1},{2,18},{18,2},{3,19},{19,3},{4,20},{20... | collective-permute-start | bytes 589832 | tf_op jit(solution)/shard_map/ppermute | solution.py:19
  143.2 14.5 %collective-permute-start.39 = (bf16[2,4,16,768]{3,2,1,0:T(8,128)(2,1)S(1)}, bf16[2,4,16,768]{3,2,1,0:T(8,128)(2,1)S(1)}, u32[]{:S(2)}, u32[]{:S(2)}) collective-permute-start(bf16[2,4,16,768]{3,2,1,0:T(8,128)(2,1)S(1)} %pad_maximum_fusion.16), channel_id=1, source_target_pairs={{0,1},{1,0},{2,3},{3,2},{4,5},{5,4},{6,7},{7,6},{8,9},{9,8},{10,11... | collective-permute-start | bytes 589832 | tf_op jit(solution)/shard_map/ppermute | solution.py:19
  160.2 13.8 %collective-permute-start.45 = (bf16[4,32,768]{2,1,0:T(8,128)(2,1)S(1)}, bf16[4,32,768]{2,1,0:T(8,128)(2,1)S(1)}, u32[]{:S(2)}, u32[]{:S(2)}) collective-permute-start(bf16[4,32,768]{2,1,0:T(8,128)(2,1)S(1)} %collective-permute-done.37.refs_3_), channel_id=1, source_target_pairs={{0,16},{16,0},{1,17},{17,1},{2,18},{18,2},{3,19},{19,3},{4,20},{20... | collective-permute-start | bytes 589832 | tf_op jit(solution)/shard_map/ppermute | solution.py:19
  160.2 13.8 %collective-permute-start.43 = (bf16[4,32,768]{2,1,0:T(8,128)(2,1)S(1)}, bf16[4,32,768]{2,1,0:T(8,128)(2,1)S(1)}, u32[]{:S(2)}, u32[]{:S(2)}) collective-permute-start(bf16[4,32,768]{2,1,0:T(8,128)(2,1)S(1)} %collective-permute-done.38.refs_4_), channel_id=1, source_target_pairs={{0,2},{4,0},{8,4},{12,8},{14,12},{10,14},{6,10},{2,6},{1,3},{5,1},... | collective-permute-start | bytes 589832 | tf_op jit(solution)/shard_map/ppermute | solution.py:70
  160.6 13.4 %collective-permute-start.46 = (bf16[4,32,768]{2,1,0:T(8,128)(2,1)S(1)}, bf16[4,32,768]{2,1,0:T(8,128)(2,1)S(1)}, u32[]{:S(2)}, u32[]{:S(2)}) collective-permute-start(bf16[4,32,768]{2,1,0:T(8,128)(2,1)S(1)} %collective-permute-done.38.refs_4_), channel_id=1, source_target_pairs={{0,16},{16,0},{1,17},{17,1},{2,18},{18,2},{3,19},{19,3},{4,20},{20... | collective-permute-start | bytes 589832 | tf_op jit(solution)/shard_map/ppermute | solution.py:19
  174.8 23.4 %collective-permute-start.51 = (bf16[4,32,768]{2,1,0:T(8,128)(2,1)S(1)}, bf16[4,32,768]{2,1,0:T(8,128)(2,1)S(1)}, u32[]{:S(2)}, u32[]{:S(2)}) collective-permute-start(bf16[4,32,768]{2,1,0:T(8,128)(2,1)S(1)} %collective-permute-done.42.refs_5_), channel_id=1, source_target_pairs={{0,16},{16,0},{1,17},{17,1},{2,18},{18,2},{3,19},{19,3},{4,20},{20... | collective-permute-start | bytes 589832 | tf_op jit(solution)/shard_map/ppermute | solution.py:19
  175.9 22.4 %collective-permute-start.52 = (bf16[4,32,768]{2,1,0:T(8,128)(2,1)S(1)}, bf16[4,32,768]{2,1,0:T(8,128)(2,1)S(1)}, u32[]{:S(2)}, u32[]{:S(2)}) collective-permute-start(bf16[4,32,768]{2,1,0:T(8,128)(2,1)S(1)} %collective-permute-done.43.refs_6_), channel_id=1, source_target_pairs={{0,16},{16,0},{1,17},{17,1},{2,18},{18,2},{3,19},{19,3},{4,20},{20... | collective-permute-start | bytes 589832 | tf_op jit(solution)/shard_map/ppermute | solution.py:19
  176.0 22.3 %collective-permute-start.49 = (bf16[4,16,768]{2,1,0:T(8,128)(2,1)S(1)}, bf16[4,16,768]{2,1,0:T(8,128)(2,1)S(1)}, u32[]{:S(2)}, u32[]{:S(2)}) collective-permute-start(bf16[4,16,768]{2,1,0:T(8,128)(2,1)S(1)} %get-tuple-element.386), channel_id=1, source_target_pairs={{0,2},{4,0},{8,4},{12,8},{14,12},{10,14},{6,10},{2,6},{1,3},{5,1},... | collective-permute-start | bytes 294920 | tf_op jit(solution)/shard_map/ppermute | solution.py:70
  177.2 21.0 %collective-permute-start.50 = (bf16[2,4,16,768]{3,2,1,0:T(8,128)(2,1)S(1)}, bf16[2,4,16,768]{3,2,1,0:T(8,128)(2,1)}, u32[]{:S(2)}, u32[]{:S(2)}) collective-permute-start(bf16[2,4,16,768]{3,2,1,0:T(8,128)(2,1)S(1)} %pad_maximum_fusion.18), channel_id=1, source_target_pairs={{0,1},{1,0},{2,3},{3,2},{4,5},{5,4},{6,7},{7,6},{8,9},{9,8},{10,11... | collective-permute-start | bytes 589832 | tf_op jit(solution)/shard_map/ppermute | solution.py:19
  180.4 17.9 %collective-permute-start.53 = (bf16[2,4,16,768]{3,2,1,0:T(8,128)(2,1)S(1)}, bf16[2,4,16,768]{3,2,1,0:T(8,128)(2,1)S(1)}, u32[]{:S(2)}, u32[]{:S(2)}) collective-permute-start(bf16[2,4,16,768]{3,2,1,0:T(8,128)(2,1)S(1)} %collective-permute-done.44.refs_9_), channel_id=1, source_target_pairs={{0,16},{16,0},{1,17},{17,1},{2,18},{18,2},{3,19},{19,3},{4,20},{20... | collective-permute-start | bytes 589832 | tf_op jit(solution)/shard_map/ppermute | solution.py:19
  302.5 348.9 %reduce-scatter.5.cloned.1.call-start = ((), (), s32[]{:S(2)}) async-start(), calls=%async_computation.5 | async-start | bytes 9732096 | tf_op jit(solution)/shard_map/reduce_scatter | solution.py:335
  329.8 33.0 %collective-permute-start.61 = (bf16[2,512,768]{2,1,0:T(8,128)(2,1)}, bf16[2,512,768]{2,1,0:T(8,128)(2,1)S(1)}, u32[]{:S(2)}, u32[]{:S(2)}) collective-permute-start(bf16[2,512,768]{2,1,0:T(8,128)(2,1)} %get-tuple-element.217), channel_id=1, source_target_pairs={{0,16},{16,0},{1,17},{17,1},{2,18},{18,2},{3,19},{19,3},{4,20},{20... | collective-permute-start | bytes 4718600 | tf_op jit(solution)/shard_map/ppermute | solution.py:19
  341.8 19.7 %collective-permute-start.59 = (bf16[512,768]{1,0:T(8,128)(2,1)}, bf16[512,768]{1,0:T(8,128)(2,1)}, u32[]{:S(2)}, u32[]{:S(2)}) collective-permute-start(bf16[512,768]{1,0:T(8,128)(2,1)} %multiply_convert_fusion), channel_id=1, source_target_pairs={{1,16},{16,1},{3,18},{18,3},{5,20},{20,5},{7,22},{22,7},{9,24},{24... | collective-permute-start | bytes 2359304 | tf_op jit(solution)/shard_map/ppermute | solution.py:23
  377.7 55.8 %collective-permute-start.62 = (bf16[8,4,48,768]{3,2,1,0:T(8,128)(2,1)}, bf16[8,4,48,768]{3,2,1,0:T(8,128)(2,1)}, u32[]{:S(2)}, u32[]{:S(2)}) collective-permute-start(bf16[8,4,48,768]{3,2,1,0:T(8,128)(2,1)} %pad_maximum_fusion.3), channel_id=1, source_target_pairs={{0,16},{16,0},{1,17},{17,1},{2,18},{18,2},{3,19},{19,3},{4,20},{20... | collective-permute-start | bytes 7077896 | tf_op jit(solution)/shard_map/ppermute | solution.py:19
  380.6 33.8 %collective-permute-start.70 = (f32[4608]{0:T(1024)S(1)}, f32[4608]{0:T(1024)S(1)}, u32[]{:S(2)}, u32[]{:S(2)}) collective-permute-start(f32[4608]{0:T(1024)S(1)} %constant_dynamic-update-slice_fusion.8), channel_id=1, source_target_pairs={{0,16},{16,0},{1,17},{17,1},{2,18},{18,2},{3,19},{19,3},{4,20},{20... | collective-permute-start | bytes 55304 | tf_op jit(solution)/shard_map/ppermute | solution.py:19
  431.1 37.2 %collective-permute-start.74 = (bf16[8,4608]{1,0:T(8,128)(2,1)S(1)}, bf16[8,4608]{1,0:T(8,128)(2,1)S(1)}, u32[]{:S(2)}, u32[]{:S(2)}) collective-permute-start(bf16[8,4608]{1,0:T(8,128)(2,1)S(1)} %maximum_select_fusion.8), channel_id=1, source_target_pairs={{0,1},{1,0},{2,3},{3,2},{4,5},{5,4},{6,7},{7,6},{8,9},{9,8},{10,11... | collective-permute-start | bytes 221192 | tf_op jit(solution)/shard_map/ppermute | solution.py:28
  439.5 27.4 %collective-permute-start.63 = (bf16[1,4,16,768]{3,2,1,0:T(8,128)(2,1)S(1)}, bf16[1,4,16,768]{3,2,1,0:T(8,128)(2,1)S(1)}, u32[]{:S(2)}, u32[]{:S(2)}) collective-permute-start(bf16[1,4,16,768]{3,2,1,0:T(8,128)(2,1)S(1)} %get-tuple-element.332), channel_id=1, source_target_pairs={{0,1},{1,0},{2,3},{3,2},{4,5},{5,4},{6,7},{7,6},{8,9},{9,8},{10,11... | collective-permute-start | bytes 294920 | tf_op jit(solution)/shard_map/ppermute | solution.py:19
  439.7 27.2 %collective-permute-start.64 = (bf16[2,4,16,768]{3,2,1,0:T(8,128)(2,1)S(1)}, bf16[2,4,16,768]{3,2,1,0:T(8,128)(2,1)S(1)}, u32[]{:S(2)}, u32[]{:S(2)}) collective-permute-start(bf16[2,4,16,768]{3,2,1,0:T(8,128)(2,1)S(1)} %pad_maximum_fusion.19), channel_id=1, source_target_pairs={{0,1},{1,0},{2,3},{3,2},{4,5},{5,4},{6,7},{7,6},{8,9},{9,8},{10,11... | collective-permute-start | bytes 589832 | tf_op jit(solution)/shard_map/ppermute | solution.py:19
  468.3 17.7 %collective-permute-start.65 = (bf16[2,512,768]{2,1,0:T(8,128)(2,1)S(1)}, bf16[2,512,768]{2,1,0:T(8,128)(2,1)S(1)}, u32[]{:S(2)}, u32[]{:S(2)}) collective-permute-start(bf16[2,512,768]{2,1,0:T(8,128)(2,1)S(1)} %get-tuple-element.239), channel_id=1, source_target_pairs={{0,16},{16,0},{1,17},{17,1},{2,18},{18,2},{3,19},{19,3},{4,20},{20... | collective-permute-start | bytes 4718600 | tf_op jit(solution)/shard_map/ppermute | solution.py:19
  472.1 24.2 %collective-permute-start.68 = (bf16[2,4,16,768]{3,2,1,0:T(8,128)(2,1)}, bf16[2,4,16,768]{3,2,1,0:T(8,128)(2,1)}, u32[]{:S(2)}, u32[]{:S(2)}) collective-permute-start(bf16[2,4,16,768]{3,2,1,0:T(8,128)(2,1)} %pad_maximum_fusion.20), channel_id=1, source_target_pairs={{0,1},{1,0},{2,3},{3,2},{4,5},{5,4},{6,7},{7,6},{8,9},{9,8},{10,11... | collective-permute-start | bytes 589832 | tf_op jit(solution)/shard_map/ppermute | solution.py:19
  474.8 128.8 %collective-permute-start.106 = (bf16[1,4,16,768]{3,2,1,0:T(8,128)(2,1)}, bf16[1,4,16,768]{3,2,1,0:T(8,128)(2,1)}, u32[]{:S(2)}, u32[]{:S(2)}) collective-permute-start(bf16[1,4,16,768]{3,2,1,0:T(8,128)(2,1)} %get-tuple-element.325), channel_id=1, source_target_pairs={{0,1},{1,0},{2,3},{3,2},{4,5},{5,4},{6,7},{7,6},{8,9},{9,8},{10,11... | collective-permute-start | bytes 294920 | tf_op jit(solution)/shard_map/ppermute | solution.py:19
  477.5 18.8 %collective-permute-start.66 = (bf16[4,16,768]{2,1,0:T(8,128)(2,1)S(1)}, bf16[4,16,768]{2,1,0:T(8,128)(2,1)S(1)}, u32[]{:S(2)}, u32[]{:S(2)}) collective-permute-start(bf16[4,16,768]{2,1,0:T(8,128)(2,1)S(1)} %get-tuple-element.382), channel_id=1, source_target_pairs={{0,4},{4,8},{8,12},{12,14},{14,10},{10,6},{6,2},{2,0},{1,5},{5,9},... | collective-permute-start | bytes 294920 | tf_op jit(solution)/shard_map/ppermute | solution.py:70
  497.3 71.7 %collective-permute-start.69 = (bf16[512,768]{1,0:T(8,128)(2,1)}, bf16[512,768]{1,0:T(8,128)(2,1)S(1)}, u32[]{:S(2)}, u32[]{:S(2)}) collective-permute-start(bf16[512,768]{1,0:T(8,128)(2,1)} %convert_element_type.430), channel_id=1, source_target_pairs={{1,16},{16,1},{3,18},{18,3},{5,20},{20,5},{7,22},{22,7},{9,24},{24... | collective-permute-start | bytes 2359304 | tf_op jit(solution)/shard_map/ppermute | solution.py:23
  499.8 35.8 %collective-permute-start.90 = (bf16[4,32,768]{2,1,0:T(8,128)(2,1)S(1)}, bf16[4,32,768]{2,1,0:T(8,128)(2,1)}, u32[]{:S(2)}, u32[]{:S(2)}) collective-permute-start(bf16[4,32,768]{2,1,0:T(8,128)(2,1)S(1)} %pad_maximum_fusion.24), channel_id=1, source_target_pairs={{0,2},{4,0},{8,4},{12,8},{14,12},{10,14},{6,10},{2,6},{1,3},{5,1},... | collective-permute-start | bytes 589832 | tf_op jit(solution)/shard_map/ppermute | solution.py:70
  524.5 51.7 %collective-permute-start.83 = (bf16[8,4,48,768]{3,2,1,0:T(8,128)(2,1)}, bf16[8,4,48,768]{3,2,1,0:T(8,128)(2,1)}, u32[]{:S(2)}, u32[]{:S(2)}) collective-permute-start(bf16[8,4,48,768]{3,2,1,0:T(8,128)(2,1)} %pad_maximum_fusion.4), channel_id=1, source_target_pairs={{0,16},{16,0},{1,17},{17,1},{2,18},{18,2},{3,19},{19,3},{4,20},{20... | collective-permute-start | bytes 7077896 | tf_op jit(solution)/shard_map/ppermute | solution.py:19
  537.4 18.2 %collective-permute-start.91 = (bf16[4,32,768]{2,1,0:T(8,128)(2,1)}, bf16[4,32,768]{2,1,0:T(8,128)(2,1)S(1)}, u32[]{:S(2)}, u32[]{:S(2)}) collective-permute-start(bf16[4,32,768]{2,1,0:T(8,128)(2,1)} %add_convert_fusion.9), channel_id=1, source_target_pairs={{0,2},{4,0},{8,4},{12,8},{14,12},{10,14},{6,10},{2,6},{1,3},{5,1},... | collective-permute-start | bytes 589832 | tf_op jit(solution)/shard_map/ppermute | solution.py:70
  538.8 16.7 %collective-permute-start.82 = (f32[4,8,96]{2,1,0:T(8,128)S(1)}, f32[4,8,96]{2,1,0:T(8,128)S(1)}, u32[]{:S(2)}, u32[]{:S(2)}) collective-permute-start(f32[4,8,96]{2,1,0:T(8,128)S(1)} %maximum_select_fusion.13), channel_id=1, source_target_pairs={{0,8},{2,10},{4,12},{6,14},{8,0},{10,2},{12,4},{14,6},{1,9},{3,11}... | collective-permute-start | bytes 36872 | tf_op jit(solution)/shard_map/ppermute | solution.py:28
  557.7 36.9 %collective-permute-start.92 = (bf16[4,32,768]{2,1,0:T(8,128)(2,1)S(1)}, bf16[4,32,768]{2,1,0:T(8,128)(2,1)S(1)}, u32[]{:S(2)}, u32[]{:S(2)}) collective-permute-start(bf16[4,32,768]{2,1,0:T(8,128)(2,1)S(1)} %get-tuple-element.333), channel_id=1, source_target_pairs={{0,2},{4,0},{8,4},{12,8},{14,12},{10,14},{6,10},{2,6},{1,3},{5,1},... | collective-permute-start | bytes 589832 | tf_op jit(solution)/shard_map/ppermute | solution.py:70
  575.8 25.4 %collective-permute-start.89 = (bf16[4,32,768]{2,1,0:T(8,128)(2,1)S(1)}, bf16[4,32,768]{2,1,0:T(8,128)(2,1)S(1)}, u32[]{:S(2)}, u32[]{:S(2)}) collective-permute-start(bf16[4,32,768]{2,1,0:T(8,128)(2,1)S(1)} %add_convert_fusion.10), channel_id=1, source_target_pairs={{0,4},{4,8},{8,12},{12,14},{14,10},{10,6},{6,2},{2,0},{1,5},{5,9},... | collective-permute-start | bytes 589832 | tf_op jit(solution)/shard_map/ppermute | solution.py:70
  601.2 38.8 %collective-permute-start.84 = (bf16[1,4,16,768]{3,2,1,0:T(8,128)(2,1)}, bf16[1,4,16,768]{3,2,1,0:T(8,128)(2,1)}, u32[]{:S(2)}, u32[]{:S(2)}) collective-permute-start(bf16[1,4,16,768]{3,2,1,0:T(8,128)(2,1)} %get-tuple-element.313), channel_id=1, source_target_pairs={{0,1},{1,0},{2,3},{3,2},{4,5},{5,4},{6,7},{7,6},{8,9},{9,8},{10,11... | collective-permute-start | bytes 294920 | tf_op jit(solution)/shard_map/ppermute | solution.py:19
  607.1 18.6 %collective-permute-start.116 = (bf16[1,192,768]{2,1,0:T(8,128)(2,1)S(1)}, bf16[1,192,768]{2,1,0:T(8,128)(2,1)S(1)}, u32[]{:S(2)}, u32[]{:S(2)}) collective-permute-start(bf16[1,192,768]{2,1,0:T(8,128)(2,1)S(1)} %bitcast.282), channel_id=1, source_target_pairs={{0,1},{1,0},{2,3},{3,2},{4,5},{5,4},{6,7},{7,6},{8,9},{9,8},{10,11... | collective-permute-start | bytes 884744 | tf_op jit(solution)/shard_map/ppermute | solution.py:28
  625.8 14.0 %collective-permute-start.117 = (bf16[2,192,768]{2,1,0:T(8,128)(2,1)S(1)}, bf16[2,192,768]{2,1,0:T(8,128)(2,1)S(1)}, u32[]{:S(2)}, u32[]{:S(2)}) collective-permute-start(bf16[2,192,768]{2,1,0:T(8,128)(2,1)S(1)} %maximum_select_fusion.5), channel_id=1, source_target_pairs={{0,16},{16,0},{1,17},{17,1},{2,18},{18,2},{3,19},{19,3},{4,20},{20... | collective-permute-start | bytes 1769480 | tf_op jit(solution)/shard_map/ppermute | solution.py:28
  625.8 14.2 %collective-permute-start.100 = (bf16[4,32,768]{2,1,0:T(8,128)(2,1)S(1)}, bf16[4,32,768]{2,1,0:T(8,128)(2,1)S(1)}, u32[]{:S(2)}, u32[]{:S(2)}) collective-permute-start(bf16[4,32,768]{2,1,0:T(8,128)(2,1)S(1)} %get-tuple-element.321), channel_id=1, source_target_pairs={{0,4},{4,8},{8,12},{12,14},{14,10},{10,6},{6,2},{2,0},{1,5},{5,9},... | collective-permute-start | bytes 589832 | tf_op jit(solution)/shard_map/ppermute | solution.py:70
  (241 other events, 1812.8 us)
Sparse Core Ops, SparseCore 0:
  15.4 98.9 all-gather.2
  131.8 92.9 all-gather.4
  302.6 153.1 reduce-scatter.2
  475.2 147.7 reduce-scatter.4
where the time goes:
time: 687 us; the launch traced here: 675 us
  Pallas kernels  188 us (27%)
  waiting for transfers between devices  147 us (21%)
  starting transfers between devices  145 us (21%)
  local copies, waits for them, and re-layouts  91.1 us (13%)
  other arithmetic  61.5 us (9%)
  between operations  34.4 us (5%)
  matrix products  7.53 us (1%)
    ppermute x32, waiting for transfers between devices, ring_step(): lax.ppermute(value, 'shard', [(order[at], order[(at + step) % size]) for...  60.3 us
    ppermute x54, starting transfers between devices, swap_pairs(): return lax.ppermute(value, axis, [(0, 1), (1, 0)])  49.3 us
    pallas_call x2, Pallas kernels, mlp_back(): pl.pallas_call(mlp_back_kernel, grid=(parts,), in_specs=[token, token, wh...  48.7 us
    ppermute x28, starting transfers between devices, cube_pairs(): lax.ppermute(value, axis, [(at, at ^ bit) for at in range(lax.axis_size(a...  46.9 us
    unnamed x353, local copies, waits for them, and re-layouts  46.3 us
    pallas_call x2, Pallas kernels, attend_back(): pl.pallas_call(functools.partial(attend_back_kernel, width // HEADS), gri...  45.9 us
    ppermute x28, waiting for transfers between devices, cube_pairs(): lax.ppermute(value, axis, [(at, at ^ bit) for at in range(lax.axis_size(a...  45.9 us
    ppermute x32, starting transfers between devices, ring_step(): lax.ppermute(value, 'shard', [(order[at], order[(at + step) % size]) for...  43.8 us
  transfers between devices with their start and end apart: 122, of which 42 were waited for; matrix products, arithmetic and copies ran while one was open for 15% of the time, Pallas kernels for 22%

commit v1 on v0

--- a/solution.py
+++ b/solution.py
@@ -1004,6 +1004,7 @@
 
     bias_grads = [None] * LAYERS
     ada_w_grads = [None] * LAYERS
+    grad_mods = [None] * LAYERS
     ada_b_grads = [None] * LAYERS
     grad_cond = 0.0
     for layer in reversed(range(LAYERS)):
@@ -1016,8 +1017,13 @@
             functools.partial(send_mlp, layer),
             functools.partial(send_attn, layer),
         )
-        grad_mod = (grad_mod + swap_pairs(grad_mod, "rep")).astype(BF16)
-        all_mod = cube_gather(grad_mod, ("seq", "shard"))
+        grad_mods[layer] = grad_mod
+
+    both_mods = jnp.stack(grad_mods)
+    both_mods = (both_mods + swap_pairs(both_mods, "rep")).astype(BF16)
+    both_mods = cube_gather(both_mods, ("seq", "shard"))
+    for layer in range(LAYERS):
+        all_mod = both_mods[:, layer]
         ada_w_grads[layer] = dot(cond_rows, all_mod, (0,), (0,))
         own_mod = lax.dynamic_slice(
             all_mod, (0, shard * ada_bias.shape[1]), (all_mod.shape[0], ada_bias.shape[1])
@@ -1041,9 +1047,9 @@
         bias_total[:, ends[at] - ends[1] : ends[at + 1] - ends[1]] for at in range(1, 5)
     ]
     if rings:
-        moved, lates = moves.finish({3: shares[0], 8: shares[1]})
+        moved, lates = moves.finish({3: shares[0], 7: shares[1]})
         done.update(moved)
-        for layer, step in ((1, 3), (0, 8)):
+        for layer, step in ((1, 3), (0, 7)):
             spread = cube_gather(lates[step], ("rep", "seq"))
             done["mlp", layer] = spread.reshape(-1, own_rows, width).astype(F32)
     weight_grads = []

time: 687 us -> 688 us (level)
  waiting for transfers between devices: 147 us -> 131 us
  local copies, waits for them, and re-layouts: 91.1 us -> 101 us
    ppermute x4, starting transfers between devices: 4.52 us -> 13 us  [swap_layout(): moved = lax.ppermute(value, ('rep', 'seq'), [(1, 2), (2, 1)])]
    ppermute x28 -> x24, starting transfers between devices: 46.9 us -> 39.8 us  [cube_pairs(): lax.ppermute(value, axis, [(at, at ^ bit) for at in range(lax.axis_size(a...]
    ppermute x54 -> x53, waiting for transfers between devices: 40.4 us -> 34.4 us  [swap_pairs(): return lax.ppermute(value, axis, [(0, 1), (1, 0)])]
    ppermute x28 -> x24, waiting for transfers between devices: 45.9 us -> 41.4 us  [cube_pairs(): lax.ppermute(value, axis, [(at, at ^ bit) for at in range(lax.axis_size(a...]
    ppermute x54 -> x53, starting transfers between devices: 49.3 us -> 45.5 us  [swap_pairs(): return lax.ppermute(value, axis, [(0, 1), (1, 0)])]
    unnamed x353 -> x345, local copies, waits for them, and re-layouts: 46.3 us -> 47.8 us
  transfers between devices with their start and end apart: 122 -> 117, of which waited for: 42 -> 38; matrix products, arithmetic and copies ran while one was open for 15% -> 16% of each run, Pallas kernels for 22% -> 22%
where the time goes in v1:
time: 688 us; the launch traced here: 676 us
  Pallas kernels  188 us (27%)
  starting transfers between devices  147 us (21%)
  waiting for transfers between devices  131 us (19%)
  local copies, waits for them, and re-layouts  101 us (15%)
  other arithmetic  66.9 us (10%)
  between operations  35.3 us (5%)
    ppermute x32, waiting for transfers between devices, ring_step(): lax.ppermute(value, 'shard', [(order[at], order[(at + step) % size]) for...  54.8 us
    ppermute x32, starting transfers between devices, ring_step(): lax.ppermute(value, 'shard', [(order[at], order[(at + step) % size]) for...  48.7 us
    pallas_call x2, Pallas kernels, mlp_back(): pl.pallas_call(mlp_back_kernel, grid=(parts,), in_specs=[token, token, wh...  48.7 us
    unnamed x345, local copies, waits for them, and re-layouts  47.8 us
    pallas_call x2, Pallas kernels, attend_back(): pl.pallas_call(functools.partial(attend_back_kernel, width // HEADS), gri...  46 us
    ppermute x53, starting transfers between devices, swap_pairs(): return lax.ppermute(value, axis, [(0, 1), (1, 0)])  45.5 us
    ppermute x24, waiting for transfers between devices, cube_pairs(): lax.ppermute(value, axis, [(at, at ^ bit) for at in range(lax.axis_size(a...  41.4 us
    ppermute x24, starting transfers between devices, cube_pairs(): lax.ppermute(value, axis, [(at, at ^ bit) for at in range(lax.axis_size(a...  39.8 us
  transfers between devices with their start and end apart: 117, of which 38 were waited for; matrix products, arithmetic and copies ran while one was open for 16% of the time, Pallas kernels for 22%

profile of v1, /device:TPU:0, one launch (start us, length us, event | category | flops | bytes accessed | tf_op | source)
XLA Modules:
  0.0 675.6 jit_solution(15464881752504698710)
XLA Ops:
  18.2 3.1 collective-permute-start.2
  35.6 4.4 collective-permute-done.4
  53.2 5.7 collective-permute-done.10
  61.2 5.1 collective-permute-done.12.refs_6_
  67.0 4.3 collective-permute-start.18
  76.0 5.2 collective-permute-start.19
  92.2 4.0 collective-permute-start.24
  99.8 5.4 collective-permute-done.25.refs_11_
  105.4 6.5 collective-permute-start.28
  123.9 5.8 shard_map.328
  136.1 3.6 collective-permute-done.35.refs_1_
  143.5 13.5 %shard_map.329 = (bf16[512,768]{1,0:T(8,128)(2,1)S(1)}, f32[6,2,512]{2,1,0:T(2,128)S(1)}) custom-call(bf16[512,768]{1,0:T(8,128)(2,1)S(1)} %copy-done.88, bf16[2,512,768]{2,1,0:T(8,128)(2,1)} %get-tuple-element.172.own_ref, bf16[2,512,768]{2,1,0:T(8,128)(2,1)} %collective-permute-done.34.other_ref), custom_call_target="tpu_custom_call" | custom-call | flops 6442450944 | bytes 4718592 | tf_op jit(solution)/shard_map/pallas_call | solution.py:417
  162.9 5.5 collective-permute-done.42.refs_5_
  170.0 4.0 collective-permute-done.43.refs_6_
  180.2 14.4 %shard_map.330 = (f32[512,768]{1,0:T(8,128)S(1)}, f32[512,768]{1,0:T(8,128)S(1)}, bf16[512,768]{1,0:T(8,128)(2,1)S(1)}, f32[4,512,768]{2,1,0:T(8,128)}, bf16[4,5...) custom-call(bf16[512,768]{1,0:T(8,128)(2,1)S(1)} %get-tuple-element.181.mixed_ref, ...), custom_call_target="tpu_custom_call" | custom-call | flops 5435817984 | bytes 17301504 | tf_op jit(solution)/shard_map/pallas_call | solution.py:626
  199.1 3.6 collective-permute-start.54
  202.7 5.5 collective-permute-done.54.refs_11_
  221.7 3.0 shard_map.331.weight_ref.proj_ref
  226.9 5.7 shard_map.332
  239.0 13.5 %shard_map.333 = (bf16[512,768]{1,0:T(8,128)(2,1)S(1)}, f32[6,2,512]{2,1,0:T(2,128)S(1)}) custom-call(bf16[512,768]{1,0:T(8,128)(2,1)S(1)} %copy-done.91, bf16[2,512,768]{2,1,0:T(8,128)(2,1)} %get-tuple-element.200.own_ref, bf16[2,512,768]{2,1,0:T(8,128)(2,1)} %collective-permute-done.58.other_ref), custom_call_target="tpu_custom_call" | custom-call | flops 6442450944 | bytes 4718592 | tf_op jit(solution)/shard_map/pallas_call | solution.py:417
  252.6 14.6 %shard_map.334 = (f32[512,768]{1,0:T(8,128)S(1)}, f32[512,768]{1,0:T(8,128)S(1)}, bf16[512,768]{1,0:T(8,128)(2,1)S(1)}, f32[4,512,768]{2,1,0:T(8,128)}, bf16[4,5...) custom-call(bf16[512,768]{1,0:T(8,128)(2,1)S(1)} %get-tuple-element.201.mixed_ref, ...), custom_call_target="tpu_custom_call" | custom-call | flops 5435817984 | bytes 17301504 | tf_op jit(solution)/shard_map/pallas_call | solution.py:626
  270.4 24.3 %shard_map.335 = (bf16[8,4,96,768]{3,2,1,0:T(8,128)(2,1)}, bf16[8,4,96,768]{3,2,1,0:T(8,128)(2,1)}, bf16[8,1,96,768]{3,2,1,0:T(8,128)(2,1)}, f32[4,1,768]{2,1,0:...) custom-call(f32[512,768]{1,0:T(8,128)} %convert_multiply_fusion.grad_ref, ...), custom_call_target="tpu_custom_call" | custom-call | flops 10871635968 | bytes 36175872 | tf_op jit(solution)/shard_map/pallas_call | solution.py:715
  294.8 7.7 %pad_maximum_fusion = bf16[8,8,96,768]{3,2,1,0:T(8,128)(2,1)} fusion(bf16[8,4,96,768]{3,2,1,0:T(8,128)(2,1)} %get-tuple-element.211, bf16[8,4,96,768]{3,2,1,0:T(8,128)(2,1)} %get-tuple-element.210), kind=kLoop, calls=%fused_computation.1 | loop fusion | flops 4718592 | bytes 18874368 | tf_op jit(solution)/shard_map/concatenate | solution.py:993
  305.0 23.1 %shard_map.336 = (bf16[512,768]{1,0:T(8,128)(2,1)S(1)}, f32[2,512,768]{2,1,0:T(8,128)S(1)}, bf16[2,512,768]{2,1,0:T(8,128)(2,1)}) custom-call(bf16[512,768]{1,0:T(8,128)(2,1)S(1)} %copy-done.92, bf16[2,512,768]{2,1,0:T(8,128)(2,1)} %get-tuple-element.200.own_ref, bf16[2,512,768]{2,1,0:T(8,128)(2,1)} %collective-permute-done.58.other_ref, ...), custom_call_target="tpu_custom_call" | custom-call | flops 16106127360 | bytes 9437184 | tf_op jit(solution)/shard_map/pallas_call | solution.py:471
  329.8 11.0 %collective-permute-start.61 = (bf16[2,512,768]{2,1,0:T(8,128)(2,1)}, bf16[2,512,768]{2,1,0:T(8,128)(2,1)S(1)}, u32[]{:S(2)}, u32[]{:S(2)}) collective-permute-start(bf16[2,512,768]{2,1,0:T(8,128)(2,1)} %get-tuple-element.217), channel_id=1, source_target_pairs={{0,16},{16,0},{1,17},{17,1},{2,18},{18,2},{3,19},{19,3},{4,20},{20... | collective-permute-start | bytes 4718600 | tf_op jit(solution)/shard_map/ppermute | solution.py:19
  359.5 10.1 %collective-permute-start.59 = (bf16[512,768]{1,0:T(8,128)(2,1)}, bf16[512,768]{1,0:T(8,128)(2,1)}, u32[]{:S(2)}, u32[]{:S(2)}) collective-permute-start(bf16[512,768]{1,0:T(8,128)(2,1)} %multiply_convert_fusion), channel_id=1, source_target_pairs={{1,16},{16,1},{3,18},{18,3},{5,20},{20,5},{7,22},{22,7},{9,24},{24... | collective-permute-start | bytes 2359304 | tf_op jit(solution)/shard_map/ppermute | solution.py:23
  372.4 9.9 %shard_map.337 = (bf16[8,3,96,768]{3,2,1,0:T(8,128)(2,1)}, f32[2,768]{1,0:T(2,128)S(1)}, f32[3,1,768]{2,1,0:T(1,128)S(1)}, f32[512,768]{1,0:T(8,128)S(1)}) custom-call(bf16[512,768]{1,0:T(8,128)(2,1)S(1)} %get-tuple-element.215.gq_ref, f32[2,512,768]{2,1,0:T(8,128)} %copy-done.6, bf16[2,512,768]{2,1,0:T(8,128)(2,1)S(1)} %collective-permute-done.61.back_ref, ...), custom_call_target="tpu_custom_call" | custom-call | flops 3623878656 | bytes 16515072 | tf_op jit(solution)/shard_map/pallas_call | solution.py:783
  389.2 24.4 %shard_map.338 = (bf16[8,4,96,768]{3,2,1,0:T(8,128)(2,1)}, bf16[8,4,96,768]{3,2,1,0:T(8,128)(2,1)}, bf16[8,1,96,768]{3,2,1,0:T(8,128)(2,1)}, f32[4,1,768]{2,1,0:...) custom-call(f32[512,768]{1,0:T(8,128)} %copy-done.14, ...), custom_call_target="tpu_custom_call" | custom-call | flops 10871635968 | bytes 36175872 | tf_op jit(solution)/shard_map/pallas_call | solution.py:715
  413.6 7.8 %pad_maximum_fusion.1 = bf16[8,8,96,768]{3,2,1,0:T(8,128)(2,1)} fusion(bf16[8,4,96,768]{3,2,1,0:T(8,128)(2,1)} %get-tuple-element.228, bf16[8,4,96,768]{3,2,1,0:T(8,128)(2,1)} %get-tuple-element.227), kind=kLoop, calls=%fused_computation.2 | loop fusion | flops 4718592 | bytes 18874368 | tf_op jit(solution)/shard_map/concatenate | solution.py:993
  428.3 22.9 %shard_map.339 = (bf16[512,768]{1,0:T(8,128)(2,1)S(1)}, f32[2,512,768]{2,1,0:T(8,128)S(1)}, bf16[2,512,768]{2,1,0:T(8,128)(2,1)S(1)}) custom-call(bf16[512,768]{1,0:T(8,128)(2,1)S(1)} %copy-done.89, bf16[2,512,768]{2,1,0:T(8,128)(2,1)} %get-tuple-element.172.own_ref, bf16[2,512,768]{2,1,0:T(8,128)(2,1)} %collective-permute-done.34.other_ref, ...), custom_call_target="tpu_custom_call" | custom-call | flops 16106127360 | bytes 9437184 | tf_op jit(solution)/shard_map/pallas_call | solution.py:471
  475.0 3.5 collective-permute-start.66
  478.4 3.2 collective-permute-done.81
  482.7 10.3 %shard_map.340 = (bf16[8,3,96,768]{3,2,1,0:T(8,128)(2,1)}, f32[2,768]{1,0:T(2,128)S(1)}, f32[3,1,768]{2,1,0:T(1,128)S(1)}, f32[512,768]{1,0:T(8,128)S(1)}) custom-call(bf16[512,768]{1,0:T(8,128)(2,1)S(1)} %copy-done.20, f32[2,512,768]{2,1,0:T(8,128)} %copy-done.7, bf16[2,512,768]{2,1,0:T(8,128)(2,1)S(1)} %collective-permute-done.65.back_ref, ...), custom_call_target="tpu_custom_call" | custom-call | flops 3623878656 | bytes 16515072 | tf_op jit(solution)/shard_map/pallas_call | solution.py:783
  501.3 5.3 collective-permute-start.104
  518.4 3.5 constant_dynamic-slice_fusion.14
  529.6 8.6 %collective-permute-done.73 = bf16[4,2,4608]{2,1,0:T(2,128)(2,1)S(1)} collective-permute-done((bf16[4,2,4608]{2,1,0:T(2,128)(2,1)S(1)}, bf16[4,2,4608]{2,1,0:T(2,128)(2,1)S(1)}, u32[]{:S(2)}, u32[]{:S(2)}) %collective-permute-start.73) | collective-permute-done | bytes 73760 | tf_op jit(solution)/shard_map/ppermute | solution.py:28
  552.3 6.1 collective-permute-done.76
  559.1 4.0 collective-permute-done.77
  568.9 3.8 collective-permute-done.82
  575.4 4.1 collective-permute-done.83
  586.6 5.9 collective-permute-done.92
  596.4 5.6 collective-permute-done.80
  611.7 6.6 collective-permute-done.93
  620.4 4.9 collective-permute-done.94
  628.1 3.1 collective-permute-done.96
  634.7 3.5 collective-permute-done.97
  646.9 4.0 collective-permute-done.99
  654.7 7.0 %collective-permute-done.109 = bf16[1,192,768]{2,1,0:T(8,128)(2,1)S(1)} collective-permute-done((bf16[1,192,768]{2,1,0:T(8,128)(2,1)S(1)}, bf16[1,192,768]{2,1,0:T(8,128)(2,1)S(1)}, u32[]{:S(2)}, u32[]{:S(2)}) %collective-permute-start.109) | collective-permute-done | bytes 294944 | tf_op jit(solution)/shard_map/ppermute | solution.py:28
  (786 shorter events, 269.8 us)
Async XLA Ops:
  7.2 124.9 %all-gather.3.cloned.1.call-start = ((), (), s32[]{:S(2)}) async-start(), calls=%async_computation.2 | async-start | bytes 9732096 | tf_op jit(solution)/shard_map/all_gather | solution.py:170
  15.3 237.3 %all-gather.5.cloned.1.call-start = ((), (), s32[]{:S(2)}) async-start(), calls=%async_computation.3 | async-start | bytes 9732096 | tf_op jit(solution)/shard_map/all_gather | solution.py:170
  18.2 13.1 %collective-permute-start.2 = (bf16[4,32,768]{2,1,0:T(8,128)(2,1)S(1)}, bf16[4,32,768]{2,1,0:T(8,128)(2,1)S(1)}, u32[]{:S(2)}, u32[]{:S(2)}) collective-permute-start(bf16[4,32,768]{2,1,0:T(8,128)(2,1)S(1)} %constant_dynamic-slice_fusion.30), channel_id=1, source_target_pairs={{0,4},{4,8},{8,12},{12,14},{14,10},{10,6},{6,2},{2,0},{1,5},{5,9},... | collective-permute-start | bytes 589832 | tf_op jit(solution)/shard_map/ppermute | solution.py:70
  47.4 13.1 %collective-permute-start.11 = (bf16[4,32,768]{2,1,0:T(8,128)(2,1)S(1)}, bf16[4,32,768]{2,1,0:T(8,128)(2,1)S(1)}, u32[]{:S(2)}, u32[]{:S(2)}) collective-permute-start(bf16[4,32,768]{2,1,0:T(8,128)(2,1)S(1)} %collective-permute-done.5.refs_3_), channel_id=1, source_target_pairs={{0,4},{4,8},{8,12},{12,14},{14,10},{10,6},{6,2},{2,0},{1,5},{5,9},... | collective-permute-start | bytes 589832 | tf_op jit(solution)/shard_map/ppermute | solution.py:70
  50.0 16.4 %collective-permute-start.14 = (bf16[4,32,768]{2,1,0:T(8,128)(2,1)S(1)}, bf16[4,32,768]{2,1,0:T(8,128)(2,1)S(1)}, u32[]{:S(2)}, u32[]{:S(2)}) collective-permute-start(bf16[4,32,768]{2,1,0:T(8,128)(2,1)S(1)} %collective-permute-done.5.refs_3_), channel_id=1, source_target_pairs={{0,16},{16,0},{1,17},{17,1},{2,18},{18,2},{3,19},{19,3},{4,20},{20... | collective-permute-start | bytes 589832 | tf_op jit(solution)/shard_map/ppermute | solution.py:19
  52.8 13.5 %collective-permute-start.12 = (bf16[4,32,768]{2,1,0:T(8,128)(2,1)S(1)}, bf16[4,32,768]{2,1,0:T(8,128)(2,1)S(1)}, u32[]{:S(2)}, u32[]{:S(2)}) collective-permute-start(bf16[4,32,768]{2,1,0:T(8,128)(2,1)S(1)} %collective-permute-done.6.refs_4_), channel_id=1, source_target_pairs={{0,2},{4,0},{8,4},{12,8},{14,12},{10,14},{6,10},{2,6},{1,3},{5,1},... | collective-permute-start | bytes 589832 | tf_op jit(solution)/shard_map/ppermute | solution.py:70
  53.0 13.3 %collective-permute-start.15 = (bf16[4,32,768]{2,1,0:T(8,128)(2,1)S(1)}, bf16[4,32,768]{2,1,0:T(8,128)(2,1)S(1)}, u32[]{:S(2)}, u32[]{:S(2)}) collective-permute-start(bf16[4,32,768]{2,1,0:T(8,128)(2,1)S(1)} %collective-permute-done.6.refs_4_), channel_id=1, source_target_pairs={{0,16},{16,0},{1,17},{17,1},{2,18},{18,2},{3,19},{19,3},{4,20},{20... | collective-permute-start | bytes 589832 | tf_op jit(solution)/shard_map/ppermute | solution.py:19
  66.7 21.3 %collective-permute-start.21 = (bf16[4,32,768]{2,1,0:T(8,128)(2,1)S(1)}, bf16[4,32,768]{2,1,0:T(8,128)(2,1)S(1)}, u32[]{:S(2)}, u32[]{:S(2)}) collective-permute-start(bf16[4,32,768]{2,1,0:T(8,128)(2,1)S(1)} %collective-permute-done.11.refs_5_), channel_id=1, source_target_pairs={{0,16},{16,0},{1,17},{17,1},{2,18},{18,2},{3,19},{19,3},{4,20},{20... | collective-permute-start | bytes 589832 | tf_op jit(solution)/shard_map/ppermute | solution.py:19
  71.3 16.7 %collective-permute-start.22 = (bf16[4,32,768]{2,1,0:T(8,128)(2,1)S(1)}, bf16[4,32,768]{2,1,0:T(8,128)(2,1)S(1)}, u32[]{:S(2)}, u32[]{:S(2)}) collective-permute-start(bf16[4,32,768]{2,1,0:T(8,128)(2,1)S(1)} %collective-permute-done.12.refs_6_), channel_id=1, source_target_pairs={{0,16},{16,0},{1,17},{17,1},{2,18},{18,2},{3,19},{19,3},{4,20},{20... | collective-permute-start | bytes 589832 | tf_op jit(solution)/shard_map/ppermute | solution.py:19
  71.4 16.6 %collective-permute-start.20 = (bf16[2,4,16,768]{3,2,1,0:T(8,128)(2,1)S(1)}, bf16[2,4,16,768]{3,2,1,0:T(8,128)(2,1)S(1)}, u32[]{:S(2)}, u32[]{:S(2)}) collective-permute-start(bf16[2,4,16,768]{3,2,1,0:T(8,128)(2,1)S(1)} %pad_maximum_fusion.15), channel_id=1, source_target_pairs={{0,1},{1,0},{2,3},{3,2},{4,5},{5,4},{6,7},{7,6},{8,9},{9,8},{10,11... | collective-permute-start | bytes 589832 | tf_op jit(solution)/shard_map/ppermute | solution.py:19
  72.9 15.1 %collective-permute-start.23 = (bf16[2,4,16,768]{3,2,1,0:T(8,128)(2,1)S(1)}, bf16[2,4,16,768]{3,2,1,0:T(8,128)(2,1)S(1)}, u32[]{:S(2)}, u32[]{:S(2)}) collective-permute-start(bf16[2,4,16,768]{3,2,1,0:T(8,128)(2,1)S(1)} %collective-permute-done.13.refs_9_), channel_id=1, source_target_pairs={{0,16},{16,0},{1,17},{17,1},{2,18},{18,2},{3,19},{19,3},{4,20},{20... | collective-permute-start | bytes 589832 | tf_op jit(solution)/shard_map/ppermute | solution.py:19
  86.4 30.1 %collective-permute-start = (bf16[512,768]{1,0:T(8,128)(2,1)}, bf16[512,768]{1,0:T(8,128)(2,1)}, u32[]{:S(2)}, u32[]{:S(2)}) collective-permute-start(bf16[512,768]{1,0:T(8,128)(2,1)} %bitcast.293), channel_id=1, source_target_pairs={{1,16},{16,1},{3,18},{18,3},{5,20},{20,5},{7,22},{22,7},{9,24},{24... | collective-permute-start | bytes 2359304 | tf_op jit(solution)/shard_map/ppermute | solution.py:23
  92.2 13.1 %collective-permute-start.24 = (f32[4,9216]{1,0:T(4,128)S(1)}, f32[4,9216]{1,0:T(4,128)S(1)}, u32[]{:S(2)}, u32[]{:S(2)}) collective-permute-start(f32[4,9216]{1,0:T(4,128)S(1)} %broadcast_select_fusion.9), channel_id=1, source_target_pairs={{0,8},{2,10},{4,12},{6,14},{8,0},{10,2},{12,4},{14,6},{1,9},{3,11}... | collective-permute-start | bytes 442376 | tf_op jit(solution)/shard_map/ppermute | solution.py:28
  132.1 474.5 %reduce-scatter.3.cloned.1.call-start = ((), (), s32[]{:S(2)}) async-start(), calls=%async_computation.4 | async-start | bytes 9732096 | tf_op jit(solution)/shard_map/reduce_scatter | solution.py:335
  140.9 16.7 %collective-permute-start.37 = (bf16[4,32,768]{2,1,0:T(8,128)(2,1)S(1)}, bf16[4,32,768]{2,1,0:T(8,128)(2,1)S(1)}, u32[]{:S(2)}, u32[]{:S(2)}) collective-permute-start(bf16[4,32,768]{2,1,0:T(8,128)(2,1)S(1)} %collective-permute-done.35.refs_1_), channel_id=1, source_target_pairs={{0,4},{4,8},{8,12},{12,14},{14,10},{10,6},{6,2},{2,0},{1,5},{5,9},... | collective-permute-start | bytes 589832 | tf_op jit(solution)/shard_map/ppermute | solution.py:70
  142.7 15.0 %collective-permute-start.40 = (bf16[4,32,768]{2,1,0:T(8,128)(2,1)S(1)}, bf16[4,32,768]{2,1,0:T(8,128)(2,1)S(1)}, u32[]{:S(2)}, u32[]{:S(2)}) collective-permute-start(bf16[4,32,768]{2,1,0:T(8,128)(2,1)S(1)} %collective-permute-done.35.refs_1_), channel_id=1, source_target_pairs={{0,16},{16,0},{1,17},{17,1},{2,18},{18,2},{3,19},{19,3},{4,20},{20... | collective-permute-start | bytes 589832 | tf_op jit(solution)/shard_map/ppermute | solution.py:19
  142.7 14.9 %collective-permute-start.38 = (bf16[4,32,768]{2,1,0:T(8,128)(2,1)S(1)}, bf16[4,32,768]{2,1,0:T(8,128)(2,1)S(1)}, u32[]{:S(2)}, u32[]{:S(2)}) collective-permute-start(bf16[4,32,768]{2,1,0:T(8,128)(2,1)S(1)} %collective-permute-done.36.refs_2_), channel_id=1, source_target_pairs={{0,2},{4,0},{8,4},{12,8},{14,12},{10,14},{6,10},{2,6},{1,3},{5,1},... | collective-permute-start | bytes 589832 | tf_op jit(solution)/shard_map/ppermute | solution.py:70
  143.0 15.4 %collective-permute-start.41 = (bf16[4,32,768]{2,1,0:T(8,128)(2,1)S(1)}, bf16[4,32,768]{2,1,0:T(8,128)(2,1)S(1)}, u32[]{:S(2)}, u32[]{:S(2)}) collective-permute-start(bf16[4,32,768]{2,1,0:T(8,128)(2,1)S(1)} %collective-permute-done.36.refs_2_), channel_id=1, source_target_pairs={{0,16},{16,0},{1,17},{17,1},{2,18},{18,2},{3,19},{19,3},{4,20},{20... | collective-permute-start | bytes 589832 | tf_op jit(solution)/shard_map/ppermute | solution.py:19
  143.3 14.4 %collective-permute-start.39 = (bf16[2,4,16,768]{3,2,1,0:T(8,128)(2,1)S(1)}, bf16[2,4,16,768]{3,2,1,0:T(8,128)(2,1)S(1)}, u32[]{:S(2)}, u32[]{:S(2)}) collective-permute-start(bf16[2,4,16,768]{3,2,1,0:T(8,128)(2,1)S(1)} %pad_maximum_fusion.16), channel_id=1, source_target_pairs={{0,1},{1,0},{2,3},{3,2},{4,5},{5,4},{6,7},{7,6},{8,9},{9,8},{10,11... | collective-permute-start | bytes 589832 | tf_op jit(solution)/shard_map/ppermute | solution.py:19
  160.1 13.9 %collective-permute-start.45 = (bf16[4,32,768]{2,1,0:T(8,128)(2,1)S(1)}, bf16[4,32,768]{2,1,0:T(8,128)(2,1)S(1)}, u32[]{:S(2)}, u32[]{:S(2)}) collective-permute-start(bf16[4,32,768]{2,1,0:T(8,128)(2,1)S(1)} %collective-permute-done.37.refs_3_), channel_id=1, source_target_pairs={{0,16},{16,0},{1,17},{17,1},{2,18},{18,2},{3,19},{19,3},{4,20},{20... | collective-permute-start | bytes 589832 | tf_op jit(solution)/shard_map/ppermute | solution.py:19
  160.1 13.9 %collective-permute-start.43 = (bf16[4,32,768]{2,1,0:T(8,128)(2,1)S(1)}, bf16[4,32,768]{2,1,0:T(8,128)(2,1)S(1)}, u32[]{:S(2)}, u32[]{:S(2)}) collective-permute-start(bf16[4,32,768]{2,1,0:T(8,128)(2,1)S(1)} %collective-permute-done.38.refs_4_), channel_id=1, source_target_pairs={{0,2},{4,0},{8,4},{12,8},{14,12},{10,14},{6,10},{2,6},{1,3},{5,1},... | collective-permute-start | bytes 589832 | tf_op jit(solution)/shard_map/ppermute | solution.py:70
  160.6 13.4 %collective-permute-start.46 = (bf16[4,32,768]{2,1,0:T(8,128)(2,1)S(1)}, bf16[4,32,768]{2,1,0:T(8,128)(2,1)S(1)}, u32[]{:S(2)}, u32[]{:S(2)}) collective-permute-start(bf16[4,32,768]{2,1,0:T(8,128)(2,1)S(1)} %collective-permute-done.38.refs_4_), channel_id=1, source_target_pairs={{0,16},{16,0},{1,17},{17,1},{2,18},{18,2},{3,19},{19,3},{4,20},{20... | collective-permute-start | bytes 589832 | tf_op jit(solution)/shard_map/ppermute | solution.py:19
  174.8 23.0 %collective-permute-start.51 = (bf16[4,32,768]{2,1,0:T(8,128)(2,1)S(1)}, bf16[4,32,768]{2,1,0:T(8,128)(2,1)S(1)}, u32[]{:S(2)}, u32[]{:S(2)}) collective-permute-start(bf16[4,32,768]{2,1,0:T(8,128)(2,1)S(1)} %collective-permute-done.42.refs_5_), channel_id=1, source_target_pairs={{0,16},{16,0},{1,17},{17,1},{2,18},{18,2},{3,19},{19,3},{4,20},{20... | collective-permute-start | bytes 589832 | tf_op jit(solution)/shard_map/ppermute | solution.py:19
  175.7 22.1 %collective-permute-start.52 = (bf16[4,32,768]{2,1,0:T(8,128)(2,1)S(1)}, bf16[4,32,768]{2,1,0:T(8,128)(2,1)S(1)}, u32[]{:S(2)}, u32[]{:S(2)}) collective-permute-start(bf16[4,32,768]{2,1,0:T(8,128)(2,1)S(1)} %collective-permute-done.43.refs_6_), channel_id=1, source_target_pairs={{0,16},{16,0},{1,17},{17,1},{2,18},{18,2},{3,19},{19,3},{4,20},{20... | collective-permute-start | bytes 589832 | tf_op jit(solution)/shard_map/ppermute | solution.py:19
  175.8 22.0 %collective-permute-start.49 = (bf16[4,16,768]{2,1,0:T(8,128)(2,1)S(1)}, bf16[4,16,768]{2,1,0:T(8,128)(2,1)S(1)}, u32[]{:S(2)}, u32[]{:S(2)}) collective-permute-start(bf16[4,16,768]{2,1,0:T(8,128)(2,1)S(1)} %get-tuple-element.388), channel_id=1, source_target_pairs={{0,2},{4,0},{8,4},{12,8},{14,12},{10,14},{6,10},{2,6},{1,3},{5,1},... | collective-permute-start | bytes 294920 | tf_op jit(solution)/shard_map/ppermute | solution.py:70
  177.2 20.5 %collective-permute-start.50 = (bf16[2,4,16,768]{3,2,1,0:T(8,128)(2,1)S(1)}, bf16[2,4,16,768]{3,2,1,0:T(8,128)(2,1)}, u32[]{:S(2)}, u32[]{:S(2)}) collective-permute-start(bf16[2,4,16,768]{3,2,1,0:T(8,128)(2,1)S(1)} %pad_maximum_fusion.18), channel_id=1, source_target_pairs={{0,1},{1,0},{2,3},{3,2},{4,5},{5,4},{6,7},{7,6},{8,9},{9,8},{10,11... | collective-permute-start | bytes 589832 | tf_op jit(solution)/shard_map/ppermute | solution.py:19
  180.1 17.7 %collective-permute-start.53 = (bf16[2,4,16,768]{3,2,1,0:T(8,128)(2,1)S(1)}, bf16[2,4,16,768]{3,2,1,0:T(8,128)(2,1)S(1)}, u32[]{:S(2)}, u32[]{:S(2)}) collective-permute-start(bf16[2,4,16,768]{3,2,1,0:T(8,128)(2,1)S(1)} %collective-permute-done.44.refs_9_), channel_id=1, source_target_pairs={{0,16},{16,0},{1,17},{17,1},{2,18},{18,2},{3,19},{19,3},{4,20},{20... | collective-permute-start | bytes 589832 | tf_op jit(solution)/shard_map/ppermute | solution.py:19
  302.5 348.4 %reduce-scatter.5.cloned.1.call-start = ((), (), s32[]{:S(2)}) async-start(), calls=%async_computation.5 | async-start | bytes 9732096 | tf_op jit(solution)/shard_map/reduce_scatter | solution.py:335
  329.8 42.6 %collective-permute-start.61 = (bf16[2,512,768]{2,1,0:T(8,128)(2,1)}, bf16[2,512,768]{2,1,0:T(8,128)(2,1)S(1)}, u32[]{:S(2)}, u32[]{:S(2)}) collective-permute-start(bf16[2,512,768]{2,1,0:T(8,128)(2,1)} %get-tuple-element.217), channel_id=1, source_target_pairs={{0,16},{16,0},{1,17},{17,1},{2,18},{18,2},{3,19},{19,3},{4,20},{20... | collective-permute-start | bytes 4718600 | tf_op jit(solution)/shard_map/ppermute | solution.py:19
  359.5 28.3 %collective-permute-start.59 = (bf16[512,768]{1,0:T(8,128)(2,1)}, bf16[512,768]{1,0:T(8,128)(2,1)}, u32[]{:S(2)}, u32[]{:S(2)}) collective-permute-start(bf16[512,768]{1,0:T(8,128)(2,1)} %multiply_convert_fusion), channel_id=1, source_target_pairs={{1,16},{16,1},{3,18},{18,3},{5,20},{20,5},{7,22},{22,7},{9,24},{24... | collective-permute-start | bytes 2359304 | tf_op jit(solution)/shard_map/ppermute | solution.py:23
  385.4 36.0 %collective-permute-start.62 = (bf16[8,4,48,768]{3,2,1,0:T(8,128)(2,1)S(1)}, bf16[8,4,48,768]{3,2,1,0:T(8,128)(2,1)S(1)}, u32[]{:S(2)}, u32[]{:S(2)}) collective-permute-start(bf16[8,4,48,768]{3,2,1,0:T(8,128)(2,1)S(1)} %pad_maximum_fusion.3), channel_id=1, source_target_pairs={{0,16},{16,0},{1,17},{17,1},{2,18},{18,2},{3,19},{19,3},{4,20},{20... | collective-permute-start | bytes 7077896 | tf_op jit(solution)/shard_map/ppermute | solution.py:19
  425.8 28.0 %collective-permute-start.63 = (bf16[1,4,16,768]{3,2,1,0:T(8,128)(2,1)S(1)}, bf16[1,4,16,768]{3,2,1,0:T(8,128)(2,1)S(1)}, u32[]{:S(2)}, u32[]{:S(2)}) collective-permute-start(bf16[1,4,16,768]{3,2,1,0:T(8,128)(2,1)S(1)} %get-tuple-element.332), channel_id=1, source_target_pairs={{0,1},{1,0},{2,3},{3,2},{4,5},{5,4},{6,7},{7,6},{8,9},{9,8},{10,11... | collective-permute-start | bytes 294920 | tf_op jit(solution)/shard_map/ppermute | solution.py:19
  428.2 25.6 %collective-permute-start.64 = (bf16[2,4,16,768]{3,2,1,0:T(8,128)(2,1)S(1)}, bf16[2,4,16,768]{3,2,1,0:T(8,128)(2,1)S(1)}, u32[]{:S(2)}, u32[]{:S(2)}) collective-permute-start(bf16[2,4,16,768]{3,2,1,0:T(8,128)(2,1)S(1)} %pad_maximum_fusion.19), channel_id=1, source_target_pairs={{0,1},{1,0},{2,3},{3,2},{4,5},{5,4},{6,7},{7,6},{8,9},{9,8},{10,11... | collective-permute-start | bytes 589832 | tf_op jit(solution)/shard_map/ppermute | solution.py:19
  455.1 27.5 %collective-permute-start.65 = (bf16[2,512,768]{2,1,0:T(8,128)(2,1)S(1)}, bf16[2,512,768]{2,1,0:T(8,128)(2,1)S(1)}, u32[]{:S(2)}, u32[]{:S(2)}) collective-permute-start(bf16[2,512,768]{2,1,0:T(8,128)(2,1)S(1)} %get-tuple-element.239), channel_id=1, source_target_pairs={{0,16},{16,0},{1,17},{17,1},{2,18},{18,2},{3,19},{19,3},{4,20},{20... | collective-permute-start | bytes 4718600 | tf_op jit(solution)/shard_map/ppermute | solution.py:19
  469.3 23.7 %collective-permute-start.68 = (bf16[2,4,16,768]{3,2,1,0:T(8,128)(2,1)}, bf16[2,4,16,768]{3,2,1,0:T(8,128)(2,1)}, u32[]{:S(2)}, u32[]{:S(2)}) collective-permute-start(bf16[2,4,16,768]{3,2,1,0:T(8,128)(2,1)} %pad_maximum_fusion.20), channel_id=1, source_target_pairs={{0,1},{1,0},{2,3},{3,2},{4,5},{5,4},{6,7},{7,6},{8,9},{9,8},{10,11... | collective-permute-start | bytes 589832 | tf_op jit(solution)/shard_map/ppermute | solution.py:19
  472.1 134.6 %collective-permute-start.101 = (bf16[1,4,16,768]{3,2,1,0:T(8,128)(2,1)}, bf16[1,4,16,768]{3,2,1,0:T(8,128)(2,1)}, u32[]{:S(2)}, u32[]{:S(2)}) collective-permute-start(bf16[1,4,16,768]{3,2,1,0:T(8,128)(2,1)} %get-tuple-element.325), channel_id=1, source_target_pairs={{0,1},{1,0},{2,3},{3,2},{4,5},{5,4},{6,7},{7,6},{8,9},{9,8},{10,11... | collective-permute-start | bytes 294920 | tf_op jit(solution)/shard_map/ppermute | solution.py:19
  475.0 18.0 %collective-permute-start.66 = (bf16[4,16,768]{2,1,0:T(8,128)(2,1)S(1)}, bf16[4,16,768]{2,1,0:T(8,128)(2,1)S(1)}, u32[]{:S(2)}, u32[]{:S(2)}) collective-permute-start(bf16[4,16,768]{2,1,0:T(8,128)(2,1)S(1)} %get-tuple-element.384), channel_id=1, source_target_pairs={{0,4},{4,8},{8,12},{12,14},{14,10},{10,6},{6,2},{2,0},{1,5},{5,9},... | collective-permute-start | bytes 294920 | tf_op jit(solution)/shard_map/ppermute | solution.py:70
  493.1 81.0 %collective-permute-start.69 = (bf16[512,768]{1,0:T(8,128)(2,1)S(1)}, bf16[512,768]{1,0:T(8,128)(2,1)S(1)}, u32[]{:S(2)}, u32[]{:S(2)}) collective-permute-start(bf16[512,768]{1,0:T(8,128)(2,1)S(1)} %convert_element_type.429), channel_id=1, source_target_pairs={{1,16},{16,1},{3,18},{18,3},{5,20},{20,5},{7,22},{22,7},{9,24},{24... | collective-permute-start | bytes 2359304 | tf_op jit(solution)/shard_map/ppermute | solution.py:23
  494.7 21.1 %collective-permute-start.70 = (f32[2,4608]{1,0:T(2,128)}, f32[2,4608]{1,0:T(2,128)}, u32[]{:S(2)}, u32[]{:S(2)}) collective-permute-start(f32[2,4608]{1,0:T(2,128)} %pad_maximum_fusion.30), channel_id=1, source_target_pairs={{0,16},{16,0},{1,17},{17,1},{2,18},{18,2},{3,19},{19,3},{4,20},{20... | collective-permute-start | bytes 110600 | tf_op jit(solution)/shard_map/ppermute | solution.py:19
  507.5 32.3 %collective-permute-start.85 = (bf16[4,32,768]{2,1,0:T(8,128)(2,1)S(1)}, bf16[4,32,768]{2,1,0:T(8,128)(2,1)S(1)}, u32[]{:S(2)}, u32[]{:S(2)}) collective-permute-start(bf16[4,32,768]{2,1,0:T(8,128)(2,1)S(1)} %pad_maximum_fusion.24), channel_id=1, source_target_pairs={{0,2},{4,0},{8,4},{12,8},{14,12},{10,14},{6,10},{2,6},{1,3},{5,1},... | collective-permute-start | bytes 589832 | tf_op jit(solution)/shard_map/ppermute | solution.py:70
  525.6 55.5 %collective-permute-start.78 = (bf16[8,4,48,768]{3,2,1,0:T(8,128)(2,1)}, bf16[8,4,48,768]{3,2,1,0:T(8,128)(2,1)}, u32[]{:S(2)}, u32[]{:S(2)}) collective-permute-start(bf16[8,4,48,768]{3,2,1,0:T(8,128)(2,1)} %pad_maximum_fusion.4), channel_id=1, source_target_pairs={{0,16},{16,0},{1,17},{17,1},{2,18},{18,2},{3,19},{19,3},{4,20},{20... | collective-permute-start | bytes 7077896 | tf_op jit(solution)/shard_map/ppermute | solution.py:19
  541.5 22.3 %collective-permute-start.86 = (bf16[4,32,768]{2,1,0:T(8,128)(2,1)}, bf16[4,32,768]{2,1,0:T(8,128)(2,1)}, u32[]{:S(2)}, u32[]{:S(2)}) collective-permute-start(bf16[4,32,768]{2,1,0:T(8,128)(2,1)} %add_convert_fusion.9), channel_id=1, source_target_pairs={{0,2},{4,0},{8,4},{12,8},{14,12},{10,14},{6,10},{2,6},{1,3},{5,1},... | collective-permute-start | bytes 589832 | tf_op jit(solution)/shard_map/ppermute | solution.py:70
  566.9 27.9 %collective-permute-start.87 = (bf16[4,32,768]{2,1,0:T(8,128)(2,1)S(1)}, bf16[4,32,768]{2,1,0:T(8,128)(2,1)S(1)}, u32[]{:S(2)}, u32[]{:S(2)}) collective-permute-start(bf16[4,32,768]{2,1,0:T(8,128)(2,1)S(1)} %get-tuple-element.333), channel_id=1, source_target_pairs={{0,2},{4,0},{8,4},{12,8},{14,12},{10,14},{6,10},{2,6},{1,3},{5,1},... | collective-permute-start | bytes 589832 | tf_op jit(solution)/shard_map/ppermute | solution.py:70
  580.6 22.9 %collective-permute-start.84 = (bf16[4,32,768]{2,1,0:T(8,128)(2,1)S(1)}, bf16[4,32,768]{2,1,0:T(8,128)(2,1)S(1)}, u32[]{:S(2)}, u32[]{:S(2)}) collective-permute-start(bf16[4,32,768]{2,1,0:T(8,128)(2,1)S(1)} %add_convert_fusion.10), channel_id=1, source_target_pairs={{0,4},{4,8},{8,12},{12,14},{14,10},{10,6},{6,2},{2,0},{1,5},{5,9},... | collective-permute-start | bytes 589832 | tf_op jit(solution)/shard_map/ppermute | solution.py:70
  603.5 38.6 %collective-permute-start.79 = (bf16[1,4,16,768]{3,2,1,0:T(8,128)(2,1)}, bf16[1,4,16,768]{3,2,1,0:T(8,128)(2,1)}, u32[]{:S(2)}, u32[]{:S(2)}) collective-permute-start(bf16[1,4,16,768]{3,2,1,0:T(8,128)(2,1)} %get-tuple-element.313), channel_id=1, source_target_pairs={{0,1},{1,0},{2,3},{3,2},{4,5},{5,4},{6,7},{7,6},{8,9},{9,8},{10,11... | collective-permute-start | bytes 294920 | tf_op jit(solution)/shard_map/ppermute | solution.py:19
  610.2 17.6 %collective-permute-start.111 = (bf16[1,192,768]{2,1,0:T(8,128)(2,1)S(1)}, bf16[1,192,768]{2,1,0:T(8,128)(2,1)S(1)}, u32[]{:S(2)}, u32[]{:S(2)}) collective-permute-start(bf16[1,192,768]{2,1,0:T(8,128)(2,1)S(1)} %bitcast.294), channel_id=1, source_target_pairs={{0,1},{1,0},{2,3},{3,2},{4,5},{5,4},{6,7},{7,6},{8,9},{9,8},{10,11... | collective-permute-start | bytes 884744 | tf_op jit(solution)/shard_map/ppermute | solution.py:28
  627.8 14.0 %collective-permute-start.112 = (bf16[2,192,768]{2,1,0:T(8,128)(2,1)S(1)}, bf16[2,192,768]{2,1,0:T(8,128)(2,1)S(1)}, u32[]{:S(2)}, u32[]{:S(2)}) collective-permute-start(bf16[2,192,768]{2,1,0:T(8,128)(2,1)S(1)} %maximum_select_fusion.5), channel_id=1, source_target_pairs={{0,16},{16,0},{1,17},{17,1},{2,18},{18,2},{3,19},{19,3},{4,20},{20... | collective-permute-start | bytes 1769480 | tf_op jit(solution)/shard_map/ppermute | solution.py:28
  627.9 14.2 %collective-permute-start.95 = (bf16[4,32,768]{2,1,0:T(8,128)(2,1)S(1)}, bf16[4,32,768]{2,1,0:T(8,128)(2,1)S(1)}, u32[]{:S(2)}, u32[]{:S(2)}) collective-permute-start(bf16[4,32,768]{2,1,0:T(8,128)(2,1)S(1)} %get-tuple-element.321), channel_id=1, source_target_pairs={{0,4},{4,8},{8,12},{12,14},{14,10},{10,6},{6,2},{2,0},{1,5},{5,9},... | collective-permute-start | bytes 589832 | tf_op jit(solution)/shard_map/ppermute | solution.py:70
  (232 other events, 1711.5 us)
Sparse Core Ops, SparseCore 0:
  15.4 99.1 all-gather.2
  132.3 92.4 all-gather.4
  302.6 150.1 reduce-scatter.2
  472.7 152.6 reduce-scatter.4
